TPU v7x, 128 devices: a whole 4x4x4 slice. The times are simulated.
128 devices in a mesh: dp: 128 (over x, y, z, core).
Axes of the slice: x: 4, y: 4, z: 4, core: 2. Of those that a mesh axis runs over, the one named last changes fastest.
Arguments:
- tokens: bfloat16 [24576, 640], P('dp'), may hold values from -6 to 6
- segment_ids: int32 [256, 96], P('dp'), may hold values from 0 to 3, never falling along the last dimension, each value on 1 to 72 neighbouring positions
- cotangent: bfloat16 [24576, 640], P('dp'), may hold values from -6 to 6
- query_weight: bfloat16 [640, 1024], P('dp'), may hold values from -0.25 to 0.25
- key_weight: bfloat16 [640, 256], P('dp'), may hold values from -0.25 to 0.25
- value_weight: bfloat16 [640, 256], P('dp'), may hold values from -0.25 to 0.25
- out_weight: bfloat16 [1024, 640], P(None, 'dp'), may hold values from -0.1875 to 0.1875
- gate_weight: bfloat16 [640, 2048], P('dp'), may hold values from -0.25 to 0.25
- up_weight: bfloat16 [640, 2048], P('dp'), may hold values from -0.25 to 0.25
- down_weight: bfloat16 [2048, 640], P(None, 'dp'), may hold values from -0.125 to 0.125
- input_gain: bfloat16 [640], P('dp'), may hold values from 0.5 to 1.5
- query_gain: bfloat16 [256], P('dp'), may hold values from 0.5 to 1.5
- key_gain: bfloat16 [256], P('dp'), may hold values from 0.5 to 1.5
- post_attn_gain: bfloat16 [640], P('dp'), may hold values from 0.5 to 1.5
- pre_ffn_gain: bfloat16 [640], P('dp'), may hold values from 0.5 to 1.5
- post_ffn_gain: bfloat16 [640], P('dp'), may hold values from 0.5 to 1.5
Outputs:
- layer_out: bfloat16 [24576, 640], P('dp')
- grad_tokens: float32 [24576, 640], P('dp')
- grad_query_weight: float32 [640, 1024], P('dp')
- grad_key_weight: float32 [640, 256], P('dp')
- grad_value_weight: float32 [640, 256], P('dp')
- grad_out_weight: float32 [1024, 640], P(None, 'dp')
- grad_gate_weight: float32 [640, 2048], P('dp')
- grad_up_weight: float32 [640, 2048], P('dp')
- grad_down_weight: float32 [2048, 640], P(None, 'dp')
- grad_input_gain: float32 [640], P('dp')
- grad_query_gain: float32 [256], P('dp')
- grad_key_gain: float32 [256], P('dp')
- grad_post_attn_gain: float32 [640], P('dp')
- grad_pre_ffn_gain: float32 [640], P('dp')
- grad_post_ffn_gain: float32 [640], P('dp')
Inputs may be any that keep to these rules, and one draw needn't show every extreme that they name: Along each row of segment_ids the numbers never fall; each sequence is a run of 1 to 72 tokens of one row, and some sequence has exactly 72.
All inputs are finite; a program needn't handle non-finite values.
Results may differ from a plain program's by a relative error of at most 0.025.
Values may be sent and summed in bfloat16 or wider, within the bound.
A program may use at most 128 MiB of HBM per device.

v0:
```python
import math

import jax
import jax.numpy as jnp
from jax import lax
from jax.sharding import PartitionSpec as P

norm_eps = 1e-06
rope_base = 1000000.0
masked_score = -1e30


def rms_scale(signal, scale_gain):
    return (
        signal
        * lax.rsqrt(jnp.mean(signal * signal, axis=-1, keepdims=True) + norm_eps)
        * scale_gain
    )


def seg_layout(segments):
    seq_length = segments.shape[0]
    token_order = jnp.arange(seq_length, dtype=jnp.int32)
    same_seg = segments[:, None] == segments[None, :]
    earlier = token_order[None, :] < token_order[:, None]
    places = jnp.sum((same_seg & earlier).astype(jnp.int32), axis=1)
    allowed = same_seg & (token_order[None, :] <= token_order[:, None])
    return (places, allowed)


def rotate(signal, places):
    feat_width = signal.shape[-1]
    half_width = feat_width // 2
    frequency = jnp.exp(
        -math.log(rope_base) * 2.0 * jnp.arange(half_width, dtype=jnp.float32) / feat_width
    )
    angles = places.astype(jnp.float32)[:, None] * frequency[None, :]
    if signal.ndim == 3:
        angles = angles[:, None, :]
    cosine = jnp.cos(angles)
    sine_part = jnp.sin(angles)
    first_half = signal[..., :half_width]
    second_half = signal[..., half_width:]
    return jnp.concatenate(
        [
            first_half * cosine - second_half * sine_part,
            second_half * cosine + first_half * sine_part,
        ],
        axis=-1,
    )


def prep_query(query_raw, scale_gain, places):
    return rotate(rms_scale(query_raw, scale_gain), places) * query_raw.shape[-1] ** (-0.5)


def prep_key(key_raw, scale_gain, places):
    return rotate(rms_scale(key_raw, scale_gain), places)


def gated_gelu(gate_proj, up_proj):
    return jax.nn.gelu(gate_proj, approximate=True) * up_proj


def product(left, right):
    return jnp.dot(left, right, preferred_element_type=jnp.float32)


def forward_micro(params, inputs, segments):
    (
        query_weight,
        key_weight,
        value_weight,
        out_weight,
        gate_weight,
        up_weight,
        down_weight,
        input_gain,
        query_gain,
        key_gain,
        post_attn_gain,
        pre_ffn_gain,
        post_ffn_gain,
    ) = params
    row_count = inputs.shape[0]
    head_dim = key_weight.shape[1]
    head_count = query_weight.shape[1] // head_dim
    places, allowed = seg_layout(segments)
    h_first = rms_scale(inputs, input_gain.astype(jnp.float32)).astype(jnp.bfloat16)
    query_raw = product(h_first, query_weight).reshape(row_count, head_count, head_dim)
    key_raw = product(h_first, key_weight)
    values = product(h_first, value_weight).astype(jnp.bfloat16)
    queries = prep_query(query_raw, query_gain.astype(jnp.float32), places).astype(jnp.bfloat16)
    keys_rot = prep_key(key_raw, key_gain.astype(jnp.float32), places).astype(jnp.bfloat16)
    scores = jnp.einsum("rhd,cd->hrc", queries, keys_rot, preferred_element_type=jnp.float32)
    scores = jnp.where(allowed[None], scores, masked_score)
    row_max = jnp.max(scores, axis=-1, keepdims=True)
    exp_scores = jnp.exp(scores - row_max)
    row_total = jnp.sum(exp_scores, axis=-1, keepdims=True)
    attn_probs = (exp_scores / row_total).astype(jnp.bfloat16)
    log_total = row_max + jnp.log(row_total)
    context = jnp.einsum("hrc,cd->rhd", attn_probs, values, preferred_element_type=jnp.float32)
    context = context.astype(jnp.bfloat16).reshape(row_count, head_count * head_dim)
    attn_out = product(context, out_weight)
    mid_stream = inputs + rms_scale(attn_out, post_attn_gain.astype(jnp.float32))
    h_second = rms_scale(mid_stream, pre_ffn_gain.astype(jnp.float32)).astype(jnp.bfloat16)
    gate_proj = product(h_second, gate_weight)
    up_proj = product(h_second, up_weight)
    hidden = gated_gelu(gate_proj, up_proj).astype(jnp.bfloat16)
    mixed_out = product(hidden, down_weight)
    result = mid_stream + rms_scale(mixed_out, post_ffn_gain.astype(jnp.float32))
    record = (
        h_first,
        query_raw,
        key_raw,
        values,
        queries,
        keys_rot,
        log_total,
        places,
        allowed,
        context,
        attn_out,
        mid_stream,
        h_second,
        gate_proj,
        up_proj,
        hidden,
        mixed_out,
    )
    return (result, record)


def backward_micro(params, inputs, record, upstream):
    (
        query_weight,
        key_weight,
        value_weight,
        out_weight,
        gate_weight,
        up_weight,
        down_weight,
        input_gain,
        query_gain,
        key_gain,
        post_attn_gain,
        pre_ffn_gain,
        post_ffn_gain,
    ) = params
    (
        h_first,
        query_raw,
        key_raw,
        values,
        queries,
        keys_rot,
        log_total,
        places,
        allowed,
        context,
        attn_out,
        mid_stream,
        h_second,
        gate_proj,
        up_proj,
        hidden,
        mixed_out,
    ) = record
    row_count = inputs.shape[0]
    head_dim = key_weight.shape[1]
    head_count = query_weight.shape[1] // head_dim
    _, pullback = jax.vjp(rms_scale, mixed_out, post_ffn_gain.astype(jnp.float32))
    grad_mixed, grad_post_ffn = pullback(upstream)
    grad_mixed = grad_mixed.astype(jnp.bfloat16)
    grad_hidden = jnp.einsum(
        "rd,fd->rf", grad_mixed, down_weight, preferred_element_type=jnp.float32
    )
    _, pullback = jax.vjp(gated_gelu, gate_proj, up_proj)
    grad_gate, grad_up = pullback(grad_hidden)
    grad_gate = grad_gate.astype(jnp.bfloat16)
    grad_up = grad_up.astype(jnp.bfloat16)
    grad_second = jnp.einsum(
        "rf,df->rd", grad_gate, gate_weight, preferred_element_type=jnp.float32
    ) + jnp.einsum("rf,df->rd", grad_up, up_weight, preferred_element_type=jnp.float32)
    _, pullback = jax.vjp(rms_scale, mid_stream, pre_ffn_gain.astype(jnp.float32))
    grad_mid_part, grad_pre_ffn = pullback(grad_second)
    grad_mid = upstream + grad_mid_part
    _, pullback = jax.vjp(rms_scale, attn_out, post_attn_gain.astype(jnp.float32))
    grad_attn, grad_post_attn = pullback(grad_mid)
    grad_attn = grad_attn.astype(jnp.bfloat16)
    grad_context = jnp.einsum(
        "rd,qd->rq", grad_attn, out_weight, preferred_element_type=jnp.float32
    )
    grad_context = grad_context.astype(jnp.bfloat16).reshape(row_count, head_count, head_dim)
    scores = jnp.einsum("rhd,cd->hrc", queries, keys_rot, preferred_element_type=jnp.float32)
    scores = jnp.where(allowed[None], scores, masked_score)
    attn_probs = jnp.exp(scores - log_total)
    grad_probs = jnp.einsum("rhd,cd->hrc", grad_context, values, preferred_element_type=jnp.float32)
    grad_values = jnp.einsum(
        "hrc,rhd->cd",
        attn_probs.astype(jnp.bfloat16),
        grad_context,
        preferred_element_type=jnp.float32,
    ).astype(jnp.bfloat16)
    grad_scores = attn_probs * (
        grad_probs - jnp.sum(attn_probs * grad_probs, axis=-1, keepdims=True)
    )
    grad_scores = grad_scores.astype(jnp.bfloat16)
    grad_queries = jnp.einsum(
        "hrc,cd->rhd", grad_scores, keys_rot, preferred_element_type=jnp.float32
    )
    grad_keys = jnp.einsum("hrc,rhd->cd", grad_scores, queries, preferred_element_type=jnp.float32)
    _, pullback = jax.vjp(
        lambda raw_part, gain_part: prep_query(raw_part, gain_part, places),
        query_raw,
        query_gain.astype(jnp.float32),
    )
    grad_qraw, grad_qgain = pullback(grad_queries)
    _, pullback = jax.vjp(
        lambda raw_part, gain_part: prep_key(raw_part, gain_part, places),
        key_raw,
        key_gain.astype(jnp.float32),
    )
    grad_kraw, grad_kgain = pullback(grad_keys)
    grad_qraw = grad_qraw.reshape(row_count, head_count * head_dim).astype(jnp.bfloat16)
    grad_kraw = grad_kraw.astype(jnp.bfloat16)
    grad_first = (
        jnp.einsum("rq,dq->rd", grad_qraw, query_weight, preferred_element_type=jnp.float32)
        + jnp.einsum("rq,dq->rd", grad_kraw, key_weight, preferred_element_type=jnp.float32)
        + jnp.einsum("rq,dq->rd", grad_values, value_weight, preferred_element_type=jnp.float32)
    )
    _, pullback = jax.vjp(rms_scale, inputs, input_gain.astype(jnp.float32))
    grad_in_part, grad_input = pullback(grad_first)
    grad_inputs = grad_mid + grad_in_part
    saved = (
        h_first,
        grad_qraw,
        grad_kraw,
        grad_values,
        context,
        grad_attn,
        h_second,
        grad_gate,
        grad_up,
        hidden,
        grad_mixed,
    )
    width_gains = (grad_input, grad_post_attn, grad_pre_ffn, grad_post_ffn)
    head_gains = (grad_qgain, grad_kgain)
    return (grad_inputs, saved, width_gains, head_gains)


def make_rows(saved, width_gains):
    (
        h_first,
        grad_qraw,
        grad_kraw,
        grad_values,
        context,
        grad_attn,
        h_second,
        grad_gate,
        grad_up,
        hidden,
        grad_mixed,
    ) = saved
    gain_cols = jnp.stack([item for item in width_gains], axis=1)
    pieces = [
        jnp.einsum("td,tq->dq", h_first, grad_qraw, preferred_element_type=jnp.float32),
        jnp.einsum("td,tq->dq", h_first, grad_kraw, preferred_element_type=jnp.float32),
        jnp.einsum("td,tq->dq", h_first, grad_values, preferred_element_type=jnp.float32),
        jnp.einsum("td,tq->dq", grad_attn, context, preferred_element_type=jnp.float32),
        jnp.einsum("td,tq->dq", h_second, grad_gate, preferred_element_type=jnp.float32),
        jnp.einsum("td,tq->dq", h_second, grad_up, preferred_element_type=jnp.float32),
        jnp.einsum("td,tq->dq", grad_mixed, hidden, preferred_element_type=jnp.float32),
        gain_cols,
    ]
    return jnp.concatenate(pieces, axis=1)


def per_device(
    tokens,
    segment_ids,
    cotangent,
    query_weight,
    key_weight,
    value_weight,
    out_weight,
    gate_weight,
    up_weight,
    down_weight,
    input_gain,
    query_gain,
    key_gain,
    post_attn_gain,
    pre_ffn_gain,
    post_ffn_gain,
):
    micro_count = segment_ids.shape[0]
    row_count = segment_ids.shape[1]
    feat_width = tokens.shape[1]
    inputs = tokens.astype(jnp.float32).reshape(micro_count, row_count, feat_width)
    upstream = cotangent.astype(jnp.float32).reshape(micro_count, row_count, feat_width)
    held_weights = (
        lax.all_gather(query_weight, "dp", axis=0, tiled=True),
        lax.all_gather(key_weight, "dp", axis=0, tiled=True),
        lax.all_gather(value_weight, "dp", axis=0, tiled=True),
        lax.all_gather(out_weight, "dp", axis=1, tiled=True),
        lax.all_gather(gate_weight, "dp", axis=0, tiled=True),
        lax.all_gather(up_weight, "dp", axis=0, tiled=True),
        lax.all_gather(down_weight, "dp", axis=1, tiled=True),
        lax.all_gather(input_gain, "dp", axis=0, tiled=True),
        lax.all_gather(query_gain, "dp", axis=0, tiled=True),
        lax.all_gather(key_gain, "dp", axis=0, tiled=True),
        lax.all_gather(post_attn_gain, "dp", axis=0, tiled=True),
        lax.all_gather(pre_ffn_gain, "dp", axis=0, tiled=True),
        lax.all_gather(post_ffn_gain, "dp", axis=0, tiled=True),
    )
    results = []
    records = []
    for micro_index in range(micro_count):
        params = held_weights
        result, record = forward_micro(params, inputs[micro_index], segment_ids[micro_index])
        results.append(result.astype(jnp.bfloat16))
        records.append(record)
    held_weights = (
        lax.all_gather(query_weight, "dp", axis=0, tiled=True),
        lax.all_gather(key_weight, "dp", axis=0, tiled=True),
        lax.all_gather(value_weight, "dp", axis=0, tiled=True),
        lax.all_gather(out_weight, "dp", axis=1, tiled=True),
        lax.all_gather(gate_weight, "dp", axis=0, tiled=True),
        lax.all_gather(up_weight, "dp", axis=0, tiled=True),
        lax.all_gather(down_weight, "dp", axis=1, tiled=True),
        lax.all_gather(input_gain, "dp", axis=0, tiled=True),
        lax.all_gather(query_gain, "dp", axis=0, tiled=True),
        lax.all_gather(key_gain, "dp", axis=0, tiled=True),
        lax.all_gather(post_attn_gain, "dp", axis=0, tiled=True),
        lax.all_gather(pre_ffn_gain, "dp", axis=0, tiled=True),
        lax.all_gather(post_ffn_gain, "dp", axis=0, tiled=True),
    )
    grad_list = []
    saved_list = []
    width_sum = None
    head_sum = None
    grad_share = None
    for micro_index in range(micro_count):
        params = held_weights
        grad_inputs, saved, width_gains, head_gains = backward_micro(
            params, inputs[micro_index], records[micro_index], upstream[micro_index]
        )
        grad_list.append(grad_inputs)
        saved_list.append(saved)
        if width_sum is None:
            width_sum = width_gains
            head_sum = head_gains
        else:
            width_sum = tuple((left + right for left, right in zip(width_sum, width_gains)))
            head_sum = tuple((left + right for left, right in zip(head_sum, head_gains)))
    joined = tuple(
        (jnp.concatenate([saved[field] for saved in saved_list], axis=0) for field in range(11))
    )
    grad_share = lax.psum_scatter(
        make_rows(joined, width_sum), "dp", scatter_dimension=0, tiled=True
    )
    query_width = query_weight.shape[1]
    head_dim = key_weight.shape[1]
    hidden_width = gate_weight.shape[1]
    edges = [
        0,
        query_width,
        head_dim,
        head_dim,
        query_width,
        hidden_width,
        hidden_width,
        hidden_width,
        4,
    ]
    bounds = [sum(edges[: place + 1]) for place in range(len(edges))]
    parts = [grad_share[:, bounds[place] : bounds[place + 1]] for place in range(8)]
    grad_query_gain, grad_key_gain = (
        lax.psum_scatter(head_sum[0], "dp", scatter_dimension=0, tiled=True),
        lax.psum_scatter(head_sum[1], "dp", scatter_dimension=0, tiled=True),
    )
    gain_part = parts[7]
    layer_out = jnp.concatenate(results, axis=0)
    grad_tokens = jnp.concatenate(grad_list, axis=0)
    return (
        layer_out,
        grad_tokens,
        parts[0],
        parts[1],
        parts[2],
        parts[3].T,
        parts[4],
        parts[5],
        parts[6].T,
        gain_part[:, 0],
        grad_query_gain,
        grad_key_gain,
        gain_part[:, 1],
        gain_part[:, 2],
        gain_part[:, 3],
    )


def solution(mesh):
    in_specs = (
        P("dp", None),
        P("dp", None),
        P("dp", None),
        P("dp", None),
        P("dp", None),
        P("dp", None),
        P(None, "dp"),
        P("dp", None),
        P("dp", None),
        P(None, "dp"),
        P("dp"),
        P("dp"),
        P("dp"),
        P("dp"),
        P("dp"),
        P("dp"),
    )
    out_specs = (
        P("dp", None),
        P("dp", None),
        P("dp", None),
        P("dp", None),
        P("dp", None),
        P(None, "dp"),
        P("dp", None),
        P("dp", None),
        P(None, "dp"),
        P("dp"),
        P("dp"),
        P("dp"),
        P("dp"),
        P("dp"),
        P("dp"),
    )
    return jax.shard_map(
        per_device, mesh=mesh, in_specs=in_specs, out_specs=out_specs, check_vma=False
    )
```

profile of v0, /device:TPU:1, one launch (start us, length us, event | category | flops | bytes accessed | tf_op | source)
XLA Modules:
  0.0 660.6 jit_solution(9242124358504251090)
XLA Ops:
  12.2 1.0 convert_element_type.190
  13.2 0.9 dynamic-update-slice.1
  18.2 69.2 %all-reduce.18 = (bf16[640]{0:T(1024)(128)(2,1)S(1)}, bf16[256]{0:T(256)(128)(2,1)S(1)}, bf16[256]{0:T(256)(128)(2,1)S(1)}, bf16[640]{0:T(1024)(128)(2,1)S(1)}, ...) all-reduce(bf16[640]{0:T(1024)(128)(2,1)S(1)} %dynamic-update-slice, ...), channel_id=1, replica_groups=mesh['dp'=128] {'dp'}, use_global_device_ids=true, to_apply=%add.8 | all-reduce | flops 3072 | bytes 12288
  88.1 34.5 %all-gather = bf16[128,5,256]{2,1,0:T(8,128)(2,1)S(1)} all-gather(bf16[1,5,256]{2,1,0:T(8,128)(2,1)} %bitcast.210), channel_id=1, replica_groups=mesh['dp'=128] {'dp'}, dimensions={0}, use_global_device_ids=true | all-gather | bytes 330240 | tf_op jit(solution)/shard_map/all_gather | solution.py:307
  122.7 34.2 %all-gather.1 = bf16[128,5,256]{2,1,0:T(8,128)(2,1)S(1)} all-gather(bf16[1,5,256]{2,1,0:T(8,128)(2,1)S(1)} %bitcast.211), channel_id=1, replica_groups=mesh['dp'=128] {'dp'}, dimensions={0}, use_global_device_ids=true | all-gather | bytes 330240 | tf_op jit(solution)/shard_map/all_gather | solution.py:306
  162.0 1.1 fusion.115
  163.1 2.6 reshape.581
  168.3 0.8 multiply_subtract_fusion.1
  169.2 1.1 fusion.164
  170.3 1.1 fusion.2
  172.5 2.7 reshape.583
  179.7 34.1 %all-gather.17.cloned.1.call-done = bf16[128,5,2048]{2,1,0:T(8,128)(2,1)} async-done(((bf16[1,5,2048]{2,1,0:T(8,128)(2,1)}), bf16[128,5,2048]{2,1,0:T(8,128)(2,1)}) %all-gather.17.cloned.1.call-update) | async-done | bytes 2621456 | tf_op jit(solution)/shard_map/all_gather | solution.py:309
  213.8 4.2 reshape.585
  218.0 63.2 %all-gather.19.cloned.1.call-done = bf16[128,5,2048]{2,1,0:T(8,128)(2,1)} async-done(((bf16[1,5,2048]{2,1,0:T(8,128)(2,1)}), bf16[128,5,2048]{2,1,0:T(8,128)(2,1)}) %all-gather.19.cloned.1.call-update) | async-done | bytes 2621456 | tf_op jit(solution)/shard_map/all_gather | solution.py:310
  281.2 5.6 reshape.587
  286.8 1.6 fusion.167
  288.5 0.9 copy-done.27
  289.4 1.8 multiply_convert_fusion.3
  291.1 57.5 %all-gather.21.cloned.1.call-done = bf16[128,5,2048]{2,1,0:T(8,128)(2,1)} async-done(((bf16[1,5,2048]{2,1,0:T(8,128)(2,1)}), bf16[128,5,2048]{2,1,0:T(8,128)(2,1)}) %all-gather.21.cloned.1.call-update) | async-done | bytes 2621456 | tf_op jit(solution)/shard_map/all_gather | solution.py:311
  348.6 5.6 reshape.589
  354.2 3.0 multiply_reduce_fusion.24
  358.7 0.9 copy-done.6
  359.6 1.0 multiply_reduce_fusion.20
  360.9 0.9 fusion.52
  361.8 1.1 multiply_convert_fusion
  363.0 0.9 fusion.172
  364.3 1.1 multiply_convert_fusion.1
  365.5 0.9 fusion.170
  366.4 1.0 convolution_add_fusion.4
  367.5 1.1 multiply_reduce_fusion.7
  376.0 2.2 fusion.46
  378.3 3.3 fusion.24
  381.5 3.2 fusion.28
  384.8 3.3 fusion.32
  389.2 1.2 fusion.84
  390.9 1.1 fusion.88
  392.1 1.1 multiply_reduce_fusion.11
  393.1 0.9 add.358
  394.0 0.9 add.359
  394.9 0.9 add.360
  395.8 0.9 add.361
  396.7 26.1 %concatenate.73 = f32[640,8708]{1,0:T(8,128)} concatenate(f32[640,1024]{1,0:T(8,128)S(1)} %fusion.42, f32[640,256]{1,0:T(8,128)} %fusion.84, f32[640,256]{1,0:T(8,128)} %fusion.88, f32[640,1024]{1,0:T(8,128)} %fusion.46, f32[640,2048]{1,0:T(8,128)} %fusion.24, f32[640,2048]{1,0:T(8,128)} %fusion.28, f32[640,2048]{1,0:T(8,128)} %fusion.32, f32[640,1]{1,0:T(8,128)} %add.358, ...), dimensions={1} | concatenate | bytes 44584960 | tf_op jit(solution)/shard_map/concatenate | solution.py:278
  423.0 63.2 %all-reduce.17 = (f32[256]{0:T(256)S(1)}, f32[256]{0:T(256)S(1)}) all-reduce(f32[256]{0:T(256)S(1)} %add.344, f32[256]{0:T(256)S(1)} %add.345), channel_id=3, replica_groups=mesh['dp'=128] {'dp'}, use_global_device_ids=true, to_apply=%region_43.44.clone | all-reduce | flops 512 | bytes 4096
  489.1 158.3 %all-reduce.21.cloned.1.call-done = f32[640,8708]{1,0:T(8,128)} async-done(((f32[640,8708]{1,0:T(8,128)}), f32[640,8708]{1,0:T(8,128)}) %all-reduce.21.cloned.1.call-update) | async-done | bytes 22292496
  647.3 1.6 dynamic-slice_bitcast_fusion.1
  648.9 1.5 fusion.163
  650.4 1.8 dynamic-slice_bitcast_fusion
  652.2 1.6 dynamic-slice_reduce_fusion
  (407 shorter events, 35.9 us)
Async XLA Ops:
  7.2 115.5 %copy-start.113 = (bf16[5,256]{1,0:T(8,128)(2,1)S(1)}, bf16[5,256]{1,0:T(8,128)(2,1)}, u32[]{:S(2)}) copy-start(bf16[5,256]{1,0:T(8,128)(2,1)} %param.20) | copy-start | bytes 7684
  7.2 155.9 %all-gather.13.cloned.1.call-start = ((), (), s32[]{:S(2)}) async-start(), calls=%async_computation | async-start | bytes 2113536 | tf_op jit(solution)/shard_map/all_gather | solution.py:305
  7.9 164.6 %all-gather.15.cloned.1.call-start = ((), (), s32[]{:S(2)}) async-start(), calls=%async_computation.1 | async-start | bytes 2113536 | tf_op jit(solution)/shard_map/all_gather | solution.py:308
  8.7 205.2 %all-gather.17.cloned.1.call-start = ((), (), s32[]{:S(2)}) async-start(), calls=%async_computation.2 | async-start | bytes 4227072 | tf_op jit(solution)/shard_map/all_gather | solution.py:309
  9.4 271.8 %all-gather.19.cloned.1.call-start = ((), (), s32[]{:S(2)}) async-start(), calls=%async_computation.3 | async-start | bytes 4227072 | tf_op jit(solution)/shard_map/all_gather | solution.py:310
  10.0 338.6 %all-gather.21.cloned.1.call-start = ((), (), s32[]{:S(2)}) async-start(), calls=%async_computation.4 | async-start | bytes 4227072 | tf_op jit(solution)/shard_map/all_gather | solution.py:311
  10.6 636.7 %all-reduce.21.cloned.1.call-start = ((), (), s32[]{:S(2)}) async-start(), calls=%async_computation.5 | async-start | bytes 45219840
  10.6 151.4 %copy-start.114 = (f32[128]{0:T(128)}, f32[128]{0:T(128)S(1)}, u32[]{:S(2)}) copy-start(f32[128]{0:T(128)S(1)} %multiply_exponential_fusion) | copy-start | bytes 1540
  87.5 71.2 %copy-start.75 = (f32[640]{0:T(1024)}, f32[640]{0:T(1024)S(1)}, u32[]{:S(2)}) copy-start(f32[640]{0:T(1024)S(1)} %convert_element_type.191) | copy-start | bytes 7684
  87.6 71.9 %copy-start.122 = (f32[96]{0:T(128)}, f32[96]{0:T(128)S(1)}, u32[]{:S(2)}) copy-start(f32[96]{0:T(128)S(1)} %get-tuple-element.44) | copy-start | bytes 1156
  88.1 71.4 %copy-start.101 = (f32[96]{0:T(128)}, f32[96]{0:T(128)S(1)}, u32[]{:S(2)}) copy-start(f32[96]{0:T(128)S(1)} %fusion.132) | copy-start | bytes 1156
  88.1 71.4 %copy-start.103 = (f32[96]{0:T(128)}, f32[96]{0:T(128)S(1)}, u32[]{:S(2)}) copy-start(f32[96]{0:T(128)S(1)} %fusion.137) | copy-start | bytes 1156
  122.6 37.9 %copy-start.65 = (bf16[192,640]{1,0:T(8,128)(2,1)S(1)}, bf16[192,640]{1,0:T(8,128)(2,1)}, u32[]{:S(2)}) copy-start(bf16[192,640]{1,0:T(8,128)(2,1)} %param.18) | copy-start | bytes 737284
  122.7 39.3 %copy-start.11 = (bf16[640,256]{1,0:T(8,128)(2,1)}, bf16[640,256]{1,0:T(8,128)(2,1)S(1)}, u32[]{:S(2)}) copy-start(bf16[640,256]{1,0:T(8,128)(2,1)S(1)} %reshape.577) | copy-start | bytes 983044
  157.1 6.0 copy-start.9
  157.2 8.6 %copy-start.18 = (bf16[96,640]{1,0:T(8,128)(2,1)}, bf16[96,640]{1,0:T(8,128)(2,1)S(1)}, u32[]{:S(2)}) copy-start(bf16[96,640]{1,0:T(8,128)(2,1)S(1)} %get-tuple-element.83) | copy-start | bytes 368644
  157.2 9.0 %copy-start.20 = (bf16[96,640]{1,0:T(8,128)(2,1)}, bf16[96,640]{1,0:T(8,128)(2,1)S(1)}, u32[]{:S(2)}) copy-start(bf16[96,640]{1,0:T(8,128)(2,1)S(1)} %get-tuple-element.84) | copy-start | bytes 368644
  158.3 7.4 %copy-start.44 = (f32[96,256]{1,0:T(8,128)}, f32[96,256]{1,0:T(8,128)S(1)}, u32[]{:S(2)}) copy-start(f32[96,256]{1,0:T(8,128)S(1)} %get-tuple-element.136) | copy-start | bytes 294916
  158.7 7.1 %copy-start.46 = (f32[96,256]{1,0:T(8,128)}, f32[96,256]{1,0:T(8,128)S(1)}, u32[]{:S(2)}) copy-start(f32[96,256]{1,0:T(8,128)S(1)} %get-tuple-element.138) | copy-start | bytes 294916
  160.3 16.3 %copy-start.77 = (f32[640]{0:T(1024)}, f32[640]{0:T(1024)S(1)}, u32[]{:S(2)}) copy-start(f32[640]{0:T(1024)S(1)} %convert_element_type.202) | copy-start | bytes 7684
  160.3 7.8 %copy-start.95 = (f32[256]{0:T(256)}, f32[256]{0:T(256)S(1)}, u32[]{:S(2)}) copy-start(f32[256]{0:T(256)S(1)} %convert_element_type.197) | copy-start | bytes 3076
  160.3 5.5 copy-start.93
  160.3 5.4 copy-start.105
  160.4 5.4 copy-start.107
  160.4 5.4 copy-start.116
  160.4 5.4 copy-start.118
  160.5 18.4 %copy-start.79 = (f32[640]{0:T(1024)}, f32[640]{0:T(1024)S(1)}, u32[]{:S(2)}) copy-start(f32[640]{0:T(1024)S(1)} %convert_element_type.203) | copy-start | bytes 7684
  163.1 5.2 copy-start.62
  163.1 8.4 %copy-start.60 = (f32[96,128]{1,0:T(8,128)}, f32[96,128]{1,0:T(8,128)S(1)}, u32[]{:S(2)}) copy-start(f32[96,128]{1,0:T(8,128)S(1)} %get-tuple-element.134) | copy-start | bytes 147460
  163.1 8.5 %copy-start.69 = (bf16[96,128]{1,0:T(8,128)(2,1)}, bf16[96,128]{1,0:T(8,128)(2,1)S(1)}, u32[]{:S(2)}) copy-start(bf16[96,128]{1,0:T(8,128)(2,1)S(1)} %get-tuple-element.131) | copy-start | bytes 73732
  168.3 3.9 copy-start.66
  170.3 5.0 copy-start.29
  172.5 4.0 copy-start.42
  175.3 4.4 copy-start.2
  384.7 3.8 copy-start.45
  384.7 3.8 copy-start.47
  384.7 3.8 copy-start.94
  384.8 3.8 copy-start.106
  384.8 4.0 copy-start.129
  384.8 4.0 copy-start.131
  384.8 4.2 copy-start.10
  422.8 64.5 %copy-start.58 = (bf16[96,640]{1,0:T(8,128)(2,1)S(1)}, bf16[96,640]{1,0:T(8,128)(2,1)}, u32[]{:S(2)}) copy-start(bf16[96,640]{1,0:T(8,128)(2,1)} %get-tuple-element.93) | copy-start | bytes 368644
  422.8 64.5 %copy-start.59 = (bf16[96,640]{1,0:T(8,128)(2,1)S(1)}, bf16[96,640]{1,0:T(8,128)(2,1)}, u32[]{:S(2)}) copy-start(bf16[96,640]{1,0:T(8,128)(2,1)} %get-tuple-element.94) | copy-start | bytes 368644
  422.8 65.2 %copy-start.121 = (f32[96]{0:T(128)S(1)}, f32[96]{0:T(128)}, u32[]{:S(2)}) copy-start(f32[96]{0:T(128)} %copy-done.120) | copy-start | bytes 1156
  422.9 65.2 %copy-start.123 = (f32[96]{0:T(128)S(1)}, f32[96]{0:T(128)}, u32[]{:S(2)}) copy-start(f32[96]{0:T(128)} %copy-done.122) | copy-start | bytes 1156
  422.9 65.2 %copy-start.37 = (f32[96,640]{1,0:T(8,128)S(1)}, f32[96,640]{1,0:T(8,128)}, u32[]{:S(2)}) copy-start(f32[96,640]{1,0:T(8,128)} %copy-done.36) | copy-start | bytes 737284
  422.9 65.2 %copy-start.39 = (f32[96,640]{1,0:T(8,128)S(1)}, f32[96,640]{1,0:T(8,128)}, u32[]{:S(2)}) copy-start(f32[96,640]{1,0:T(8,128)} %copy-done.38) | copy-start | bytes 737284
  422.9 65.2 %copy-start.48 = (f32[96,640]{1,0:T(8,128)S(1)}, f32[96,640]{1,0:T(8,128)}, u32[]{:S(2)}) copy-start(f32[96,640]{1,0:T(8,128)} %get-tuple-element.160) | copy-start | bytes 737284
  (94 other events, 190.9 us)
Sparse Core Ops, SparseCore 0:
  11.2 68.9 all-gather.12
  83.3 63.0 all-gather.14
  149.6 64.1 all-gather.16
  216.9 64.3 all-gather.18
  284.2 64.3 all-gather.20
  423.0 224.2 all-reduce.20
where the time goes:
time: 663 us; the launch traced here: 661 us
  waiting for transfers between devices  316 us (48%)
  blocking collectives  201 us (30%)
  local copies, waits for them, and re-layouts  70.5 us (11%)
  matrix products  42 us (6%)
  between operations  16.4 us (2%)
  other arithmetic  14.3 us (2%)
    unnamed x7, waiting for transfers between devices  161 us
    unnamed x2, blocking collectives  132 us
    all_gather x1, waiting for transfers between devices, per_device(): lax.all_gather(up_weight, 'dp', axis=0, tiled=True)  63.2 us
    all_gather x1, waiting for transfers between devices, per_device(): lax.all_gather(down_weight, 'dp', axis=1, tiled=True)  57.5 us
    all_gather x1, blocking collectives, per_device(): lax.all_gather(value_weight, 'dp', axis=0, tiled=True)  34.5 us
    all_gather x1, blocking collectives, per_device(): lax.all_gather(key_weight, 'dp', axis=0, tiled=True)  34.2 us
    all_gather x1, waiting for transfers between devices, per_device(): lax.all_gather(gate_weight, 'dp', axis=0, tiled=True)  34.1 us
    unnamed x293, local copies, waits for them, and re-layouts  33 us
  transfers between devices with their start and end apart: 6, of which 4 were waited for; matrix products, arithmetic and copies ran while one was open for 7% of the time, Pallas kernels for 0%

commit v1 on v0

--- a/solution.py
+++ b/solution.py
@@ -1,9 +1,611 @@
+import functools
 import math
 
 import jax
 import jax.numpy as jnp
 from jax import lax
+from jax.experimental import pallas as pl
+from jax.experimental.pallas import tpu as pltpu
 from jax.sharding import PartitionSpec as P
+
+BF = jnp.bfloat16
+F32 = jnp.float32
+MESH = pl.DeviceIdType.MESH
+
+
+class Place:
+    def __init__(self):
+        me = lax.axis_index("dp")
+        self.me = me
+        self.c = lax.rem(me, 2)
+        self.z = lax.rem(lax.div(me, 2), 4)
+        self.y = lax.rem(lax.div(me, 8), 4)
+        self.x = lax.div(me, 32)
+        self.yl = lax.rem(self.y, 2)
+        self.yh = lax.div(self.y, 2)
+        self.at = {"x": self.x, "y": self.y, "z": self.z}
+
+    def device(self, x, y, z, c):
+        return ((x * 4 + y) * 4 + z) * 2 + c
+
+    def moved(self, axis, by):
+        return lax.rem(self.at[axis] + by, 4)
+
+    def peer(self, axis, by):
+        spot = dict(self.at)
+        spot[axis] = self.moved(axis, by)
+        return self.device(spot["x"], spot["y"], spot["z"], self.c)
+
+    def sibling(self):
+        return self.device(self.x, self.y, self.z, 1 - self.c)
+
+    def group_peers(self):
+        found = []
+        for dyl in range(2):
+            for dz in range(4):
+                for dc in range(2):
+                    if dyl or dz or dc:
+                        yl = lax.rem(self.yl + dyl, 2)
+                        z = lax.rem(self.z + dz, 4)
+                        c = lax.rem(self.c + dc, 2)
+                        found.append(
+                            (
+                                self.device(self.x, self.yh * 2 + yl, z, c),
+                                c * 8 + yl * 4 + z,
+                                yl * 8 + z * 2 + c,
+                            )
+                        )
+        return found
+
+    def slot(self):
+        return self.c * 8 + self.yl * 4 + self.z
+
+    def natural(self):
+        return self.yl * 8 + self.z * 2 + self.c
+
+    def greet(self):
+        others = [item[0] for item in self.group_peers()]
+        others += [self.peer("x", by) for by in (1, 2, 3)]
+        others += [
+            self.device(self.x, (1 - self.yh) * 2 + yl, self.z, self.c) for yl in range(2)
+        ]
+        barrier = pltpu.get_barrier_semaphore()
+        for other in others:
+            pl.semaphore_signal(barrier, inc=1, device_id=(other,), device_id_type=MESH)
+        pl.semaphore_wait(barrier, len(others))
+
+
+def region(select, half=None):
+    index = []
+    for axis in "xyz":
+        value = select[axis]
+        if value is None:
+            cut = half is not None
+            if axis == "y":
+                index += [pl.ds(half, 1) if cut else slice(None), slice(None)]
+            else:
+                index.append(pl.ds(2 * half, 2) if cut else slice(None))
+            half = None
+        elif axis == "y":
+            index += [lax.div(value, 2), lax.rem(value, 2)]
+        else:
+            index.append(value)
+    return tuple(index)
+
+
+def half_shape(whole):
+    shape, cut = [], True
+    for axis in "xyz":
+        if axis in whole:
+            if axis == "y":
+                shape += [1 if cut else 2, 2]
+            else:
+                shape.append(2 if cut else 4)
+            cut = False
+    return tuple(shape)
+
+
+class Sender:
+    def __init__(self, send_sems, recv_sems):
+        self.send_sems, self.recv_sems = send_sems, recv_sems
+        self.used = 0
+        self.open = []
+
+    def send(self, source, target, device):
+        copy = pltpu.make_async_remote_copy(
+            src_ref=source,
+            dst_ref=target,
+            send_sem=self.send_sems.at[self.used],
+            recv_sem=self.recv_sems.at[self.used],
+            device_id=(device,),
+            device_id_type=MESH,
+        )
+        self.used += 1
+        copy.start()
+        self.open.append(copy)
+        return copy
+
+    def finish(self):
+        for copy in self.open:
+            copy.wait_send()
+        self.open = []
+
+
+def gather_class(place, sender, ref, rows, order):
+    tail = (pl.ds(rows[0], rows[1]), slice(None))
+
+    def view(select, half=None):
+        return ref.at[(place.c,) + region(select, half) + tail]
+
+    def select_for(step, value):
+        chosen = {}
+        for at, axis in enumerate(order):
+            chosen[axis] = None if at < step else value if at == step else place.at[axis]
+        return chosen
+
+    def push(part, device):
+        return sender.send(part, part, device)
+
+    axis = order[0]
+    own = view(select_for(0, place.at[axis]))
+    first = [push(own, place.peer(axis, by)) for by in (1, 3, 2)]
+    yield
+    for copy in first:
+        copy.wait_recv()
+    twin = []
+    for step in (1, 2):
+        axis = order[step]
+        last = step == 2
+        right, left = place.peer(axis, 1), place.peer(axis, 3)
+        mine = select_for(step, place.at[axis])
+        of_right = select_for(step, place.moved(axis, 1))
+        of_left = select_for(step, place.moved(axis, 3))
+        of_far = select_for(step, place.moved(axis, 2))
+        r0 = push(view(mine, 0), right)
+        l1 = push(view(mine, 1), left)
+        r1 = push(view(mine, 1), right)
+        l0 = push(view(mine, 0), left)
+        if last:
+            twin.append(push(view(mine), place.sibling()))
+        yield
+        r0.wait_recv()
+        f0 = push(view(of_left, 0), right)
+        l1.wait_recv()
+        f1 = push(view(of_right, 1), left)
+        yield
+        r1.wait_recv()
+        if last:
+            twin.append(push(view(of_left), place.sibling()))
+        l0.wait_recv()
+        if last:
+            twin.append(push(view(of_right), place.sibling()))
+        yield
+        f0.wait_recv()
+        if last:
+            twin.append(push(view(of_far, 0), place.sibling()))
+        f1.wait_recv()
+        if last:
+            twin.append(push(view(of_far, 1), place.sibling()))
+    yield
+    for copy in twin:
+        copy.wait_recv()
+
+
+GATHER_COPIES = 20
+SCATTER_COPIES = 19
+
+
+def scatter_class(place, sender, ref, twin_ref, landing, rows, order):
+    tail = (pl.ds(rows[0], rows[1]), slice(None))
+    order = order[::-1]
+
+    def at(select, half=None):
+        return (place.c,) + region(select, half) + tail
+
+    def select_for(step, value):
+        chosen = {}
+        for where, axis in enumerate(order):
+            chosen[axis] = (
+                place.at[axis] if where < step else value if where == step else None
+            )
+        return chosen
+
+    def add(index, *others):
+        total = ref[index].astype(F32)
+        for other in others:
+            total = total + other.astype(F32)
+        ref[index] = total.astype(BF)
+
+    axis = order[0]
+    pieces = []
+    for by in (2, 1, 3, 0):
+        part = region(select_for(0, place.moved(axis, by))) + tail
+        pieces.append(
+            (part, sender.send(ref.at[(1 - place.c,) + part], twin_ref.at[part], place.sibling()))
+        )
+    yield
+
+    def joined(which):
+        if pieces is None:
+            return
+        part, copy = pieces[which]
+        copy.wait_recv()
+        add((place.c,) + part, twin_ref[part])
+
+    for step in (0, 1):
+        axis = order[step]
+        land = landing[step]
+        right, left = place.peer(axis, 1), place.peer(axis, 3)
+        mine = select_for(step, place.at[axis])
+        to_right = select_for(step, place.moved(axis, 1))
+        to_left = select_for(step, place.moved(axis, 3))
+        far = select_for(step, place.moved(axis, 2))
+        joined(0)
+        f0 = sender.send(ref.at[at(far, 0)], land.at[0], right)
+        f1 = sender.send(ref.at[at(far, 1)], land.at[1], left)
+        joined(1)
+        r1 = sender.send(ref.at[at(to_right, 1)], land.at[2], right)
+        joined(2)
+        l0 = sender.send(ref.at[at(to_left, 0)], land.at[3], left)
+        yield
+        f0.wait_recv()
+        add(at(to_right, 0), land[0])
+        r0 = sender.send(ref.at[at(to_right, 0)], land.at[4], right)
+        f1.wait_recv()
+        add(at(to_left, 1), land[1])
+        l1 = sender.send(ref.at[at(to_left, 1)], land.at[5], left)
+        joined(3)
+        pieces = None
+        yield
+        r1.wait_recv()
+        l0.wait_recv()
+        r0.wait_recv()
+        l1.wait_recv()
+        add(at(mine, 0), land[4], land[3])
+        add(at(mine, 1), land[2], land[5])
+    axis = order[2]
+    land = landing[2]
+    sent = [
+        sender.send(
+            ref.at[at(select_for(2, place.moved(axis, by)))], land.at[by - 1], place.peer(axis, by)
+        )
+        for by in (1, 3, 2)
+    ]
+    yield
+    for copy in sent:
+        copy.wait_recv()
+    add(at(select_for(2, place.at[axis])), land[0], land[1], land[2])
+
+
+def landing_shapes(rows, order):
+    back = order[::-1]
+    return [
+        pltpu.VMEM((6,) + half_shape(back[1:]) + (rows, 128), BF),
+        pltpu.VMEM((6,) + half_shape(back[2:]) + (rows, 128), BF),
+        pltpu.VMEM((3, rows, 128), BF),
+    ]
+
+
+def take_turns(tasks):
+    tasks = list(tasks)
+    while tasks:
+        still = []
+        for task in tasks:
+            try:
+                next(task)
+                still.append(task)
+            except StopIteration:
+                pass
+        tasks = still
+
+
+def picker(part, transposed=False):
+    i = lax.broadcasted_iota(jnp.int32, (80, 512), 0)
+    j = lax.broadcasted_iota(jnp.int32, (80, 512), 1)
+    n = lax.shift_right_logical(j, 5)
+    r = lax.bitwise_and(j, 7)
+    m = lax.bitwise_and(lax.shift_right_logical(j, 3), 3)
+    hit = (m == part) & (r < 5) & (i == n * 5 + r)
+    return jnp.where(hit, 1.0, 0.0).astype(BF)
+
+
+def stacked(parts):
+    pad = jnp.zeros((3, 128), F32)
+    return jnp.concatenate(
+        [item for part in parts for item in (part.astype(F32), pad)], axis=0
+    )
+
+
+CLASSES = (
+    (0, 0, 32, "xyz"),
+    (0, 32, 48, "yzx"),
+    (4, 0, 32, "zxy"),
+    (1, 0, 80, "xyz"),
+    (2, 0, 80, "yzx"),
+    (3, 0, 80, "zxy"),
+)
+BLOCK_ROWS = (80, 80, 80, 80, 32)
+
+
+def fill_messages(q, o, k, v, g, u, d, gains, msgs, kv_block):
+    for slot in range(16):
+        lanes = slice(slot * 128, slot * 128 + 128)
+        narrow = slice(slot % 8 * 128, slot % 8 * 128 + 128)
+        qo = q[:, narrow] if slot < 8 else o[:, narrow]
+        msgs[slot] = stacked([g[:, lanes], u[:, lanes], d[:, lanes], qo]).astype(BF)
+    flat = stacked([k[:, 0:128], k[:, 128:256], v[:, 0:128], v[:, 128:256]])
+    row = lax.broadcasted_iota(jnp.int32, (32, 128), 0)
+    for at, target in enumerate(GAIN_ROWS):
+        flat = jnp.where(row == target, gains[at : at + 1, :], flat)
+    kv_block[...] = flat.astype(BF)
+
+
+GAIN_ROWS = (5, 13, 21, 29, 6, 14)
+
+
+def exchange_in(place, sender, msgs, recv, bufs, kv_block):
+    copies = [
+        sender.send(msgs.at[slot], recv.at[place.natural()], device)
+        for device, slot, _ in place.group_peers()
+    ]
+    recv[place.natural()] = msgs[place.slot()]
+    spot = (place.c, place.x, place.yh, place.yl, place.z)
+    bufs[4][spot] = kv_block[...]
+    for copy in copies:
+        copy.wait_recv()
+    flat = recv[...].reshape(512, 128)
+    for part, buf in ((3, bufs[0]), (0, bufs[1]), (1, bufs[2]), (2, bufs[3])):
+        buf[spot] = jnp.dot(picker(part), flat, preferred_element_type=F32).astype(BF)
+
+
+def spread_rows(buf, row):
+    takes = []
+    for x in range(4):
+        for yh in range(2):
+            for yl in range(2):
+                both = [
+                    jnp.concatenate(
+                        [buf[c, x, yh, yl, z, row // 8 * 8 : row // 8 * 8 + 8, :] for c in range(2)], 0
+                    )
+                    for z in range(4)
+                ]
+                takes += both
+    every = jnp.concatenate(takes, axis=0)
+    i = lax.broadcasted_iota(jnp.int32, (128, 1024), 0)
+    j = lax.broadcasted_iota(jnp.int32, (128, 1024), 1)
+    pick = jnp.where(j == i * 8 + row % 8, 1.0, 0.0).astype(BF)
+    return jnp.dot(pick, every, preferred_element_type=F32)
+
+
+def gain_line(buf, row, each, width):
+    held = spread_rows(buf, row)
+    count = lax.broadcasted_iota(jnp.int32, (128, width), 0)
+    lane = lax.broadcasted_iota(jnp.int32, (128, width), 1)
+    place_in = lane - count * each
+    r = lax.broadcasted_iota(jnp.int32, (128, width), 0)
+    rep = jnp.where(lax.rem(lane, each) == r, 1.0, 0.0).astype(BF)
+    lined = jnp.dot(held.astype(BF), rep, preferred_element_type=F32)
+    lined = jnp.where((place_in >= 0) & (place_in < each), lined, 0.0)
+    return jnp.sum(lined, axis=0, keepdims=True)
+
+
+def kv_group(buf, g, part):
+    x, yh = lax.div(g, 2), lax.rem(g, 2)
+    blocks = [
+        buf[c, x, yh, yl, z] for yl in range(2) for z in range(4) for c in range(2)
+    ]
+    return jnp.dot(picker(part), jnp.concatenate(blocks, axis=0), preferred_element_type=F32)
+
+
+def gather_kernel(
+    q, k, v, o, g, u, d, gains, qo_out, g_out, u_out, d_out, kv_out, gain_out,
+    qo_buf, g_buf, u_buf, d_buf, kv_buf, msgs, recv, kv_block, send_sems, recv_sems, out_sems,
+):
+    place = Place()
+    fill_messages(q, o, k, v, g, u, d, gains, msgs, kv_block)
+    place.greet()
+    sender = Sender(send_sems, recv_sems)
+    bufs = (qo_buf, g_buf, u_buf, d_buf, kv_buf)
+    exchange_in(place, sender, msgs, recv, bufs, kv_block)
+    take_turns(
+        gather_class(place, sender, bufs[which], (first, count), order)
+        for which, first, count, order in CLASSES
+    )
+    outs = []
+    for at, (buf, out) in enumerate(((qo_buf, qo_out), (g_buf, g_out), (u_buf, u_out), (d_buf, d_out))):
+        for slot in range(16):
+            c, yl, z = slot // 8, slot // 4 % 2, slot % 4
+            copy = pltpu.make_async_copy(
+                buf.at[c, :, :, yl, z],
+                out.at[:, :, :, pl.ds(slot * 128, 128)],
+                out_sems.at[at * 16 + slot],
+            )
+            copy.start()
+            outs.append(copy)
+    for part in range(4):
+        for group in range(8):
+            kv_out[group * 80 : group * 80 + 80, part * 128 : part * 128 + 128] = kv_group(
+                kv_buf, group, part
+            ).astype(BF)
+    gain_out[...] = jnp.zeros((8, 640), F32)
+    for at, row in enumerate(GAIN_ROWS):
+        if at < 4:
+            gain_out[at : at + 1, :] = gain_line(kv_buf, row, 5, 640)
+        else:
+            gain_out[at : at + 1, 0:256] = gain_line(kv_buf, row, 2, 256)
+    for copy in outs:
+        copy.wait()
+    sender.finish()
+
+
+def gather_weights(q, k, v, o_t, g, u, d_t, gains):
+    grid = (2, 4, 2, 2, 4)
+    vm = pl.BlockSpec(memory_space=pltpu.VMEM)
+    hbm = pl.BlockSpec(memory_space=pl.ANY)
+    copies = 15 + GATHER_COPIES * len(CLASSES)
+    wide = jax.ShapeDtypeStruct((4, 2, 80, 2048), BF)
+    return pl.pallas_call(
+        gather_kernel,
+        out_shape=(wide, wide, wide, wide,
+                   jax.ShapeDtypeStruct((640, 512), BF), jax.ShapeDtypeStruct((8, 640), F32)),
+        in_specs=[vm] * 8,
+        out_specs=(hbm, hbm, hbm, hbm, vm, vm),
+        scratch_shapes=[pltpu.VMEM(grid + (rows, 128), BF) for rows in BLOCK_ROWS]
+        + [
+            pltpu.VMEM((16, 32, 128), BF),
+            pltpu.VMEM((16, 32, 128), BF),
+            pltpu.VMEM((32, 128), BF),
+            pltpu.SemaphoreType.DMA((copies,)),
+            pltpu.SemaphoreType.DMA((copies,)),
+            pltpu.SemaphoreType.DMA((64,)),
+        ],
+        compiler_params=pltpu.CompilerParams(
+            collective_id=0, has_side_effects=True, vmem_limit_bytes=56 << 20
+        ),
+    )(q, k, v, o_t, g, u, d_t, gains)
+
+
+def spread_gain(line, each):
+    width = line.shape[1]
+    count = lax.broadcasted_iota(jnp.int32, (128, width), 0)
+    lane = lax.broadcasted_iota(jnp.int32, (128, width), 1)
+    inside = lane - count * each
+    kept = jnp.where((inside >= 0) & (inside < each), jnp.broadcast_to(line, (128, width)), 0.0)
+    r = lax.broadcasted_iota(jnp.int32, (width, 128), 0)
+    to = lax.broadcasted_iota(jnp.int32, (width, 128), 1)
+    pick = jnp.where(lax.rem(r, each) == to, 1.0, 0.0).astype(BF)
+    return jnp.dot(kept.astype(BF), pick, preferred_element_type=F32)
+
+
+def fill_kv_gradient(kv, gain_lines, buf):
+    gains = [spread_gain(line, 5 if at < 4 else 2) for at, line in enumerate(gain_lines)]
+    row = lax.broadcasted_iota(jnp.int32, (512, 128), 0)
+    seat = lax.bitwise_and(row, 31)
+    n = lax.broadcasted_iota(jnp.int32, (512, 16), 0)
+    m = lax.broadcasted_iota(jnp.int32, (512, 16), 1)
+    repeat = jnp.where(lax.shift_right_logical(n, 5) == m, 1.0, 0.0).astype(BF)
+    for group in range(8):
+        flat = jnp.zeros((512, 128), F32)
+        for part in range(4):
+            flat = flat + lax.dot_general(
+                picker(part), kv(group, part), (((0,), (0,)), ((), ())), preferred_element_type=F32
+            )
+        for at, target in enumerate(GAIN_ROWS):
+            own = gains[at][group * 16 : group * 16 + 16].astype(BF)
+            flat = jnp.where(
+                seat == target, jnp.dot(repeat, own, preferred_element_type=F32), flat
+            )
+        flat = flat.astype(BF)
+        for n16 in range(16):
+            yl, z, c = n16 // 8, n16 // 2 % 4, n16 % 2
+            buf[c, group // 2, group % 2, yl, z] = flat[n16 * 32 : n16 * 32 + 32]
+
+
+def exchange_out(place, sender, msgs, recv, bufs):
+    spot = (place.c, place.x, place.yh, place.yl, place.z)
+    flat = jnp.zeros((512, 128), F32)
+    for part, buf in ((3, bufs[0]), (0, bufs[1]), (1, bufs[2]), (2, bufs[3])):
+        flat = flat + lax.dot_general(
+            picker(part), buf[spot], (((0,), (0,)), ((), ())), preferred_element_type=F32
+        )
+    msgs[...] = flat.astype(BF).reshape(16, 32, 128)
+    copies = [
+        sender.send(msgs.at[natural], recv.at[place.slot()], device)
+        for device, _, natural in place.group_peers()
+    ]
+    recv[place.slot()] = msgs[place.natural()]
+    for copy in copies:
+        copy.wait_recv()
+
+
+def write_shards(place, recv, bufs, q_out, k_out, v_out, o_out, g_out, u_out, d_out, gain_out):
+    for slot in range(16):
+        part = recv[slot].astype(F32)
+        lanes = slice(slot * 128, slot * 128 + 128)
+        narrow = slice(slot % 8 * 128, slot % 8 * 128 + 128)
+        g_out[:, lanes] = part[0:5]
+        u_out[:, lanes] = part[8:13]
+        d_out[:, lanes] = part[16:21]
+        (q_out if slot < 8 else o_out)[:, narrow] = part[24:29]
+    spot = (place.c, place.x, place.yh, place.yl, place.z)
+    flat = bufs[4][spot].astype(F32)
+    k_out[:, 0:128] = flat[0:5]
+    k_out[:, 128:256] = flat[8:13]
+    v_out[:, 0:128] = flat[16:21]
+    v_out[:, 128:256] = flat[24:29]
+    gain_out[...] = jnp.concatenate(
+        [flat[row : row + 1] for row in GAIN_ROWS] + [jnp.zeros((2, 128), F32)], axis=0
+    )
+
+
+def scatter_kernel(
+    qo, g, u, d, kv, gain_lines,
+    q_out, k_out, v_out, o_out, g_out, u_out, d_out, gain_out,
+    *scratch,
+):
+    bufs, twins = scratch[0:5], scratch[5:10]
+    landings = scratch[10 : 10 + 3 * len(CLASSES)]
+    msgs, recv, send_sems, recv_sems, in_sems = scratch[10 + 3 * len(CLASSES) :]
+    place = Place()
+    ins = []
+    for at, (buf, source) in enumerate(((bufs[0], qo), (bufs[1], g), (bufs[2], u), (bufs[3], d))):
+        for slot in range(16):
+            c, yl, z = slot // 8, slot // 4 % 2, slot % 4
+            copy = pltpu.make_async_copy(
+                source.at[:, :, :, pl.ds(slot * 128, 128)],
+                buf.at[c, :, :, yl, z],
+                in_sems.at[at * 16 + slot],
+            )
+            copy.start()
+            ins.append(copy)
+    fill_kv_gradient(
+        lambda group, part: kv[group * 80 : group * 80 + 80, part * 128 : part * 128 + 128],
+        [gain_lines[at : at + 1, 0 : (640 if at < 4 else 256)] for at in range(6)],
+        bufs[4],
+    )
+    for copy in ins:
+        copy.wait()
+    place.greet()
+    sender = Sender(send_sems, recv_sems)
+    take_turns(
+        scatter_class(
+            place, sender, bufs[which], twins[which], landings[3 * at : 3 * at + 3], (first, count), order
+        )
+        for at, (which, first, count, order) in enumerate(CLASSES)
+    )
+    exchange_out(place, sender, msgs, recv, bufs)
+    write_shards(place, recv, bufs, q_out, k_out, v_out, o_out, g_out, u_out, d_out, gain_out)
+    sender.finish()
+
+
+def scatter_gradients(qo, g, u, d, kv, gain_lines):
+    vm = pl.BlockSpec(memory_space=pltpu.VMEM)
+    hbm = pl.BlockSpec(memory_space=pl.ANY)
+    copies = 15 + SCATTER_COPIES * len(CLASSES)
+    shape = lambda *dims: jax.ShapeDtypeStruct(dims, F32)
+    scratch = [pltpu.VMEM((2, 4, 2, 2, 4, rows, 128), BF) for rows in BLOCK_ROWS]
+    scratch += [pltpu.VMEM((4, 2, 2, 4, rows, 128), BF) for rows in BLOCK_ROWS]
+    for _, _, count, order in CLASSES:
+        scratch += landing_shapes(count, order)
+    return pl.pallas_call(
+        scatter_kernel,
+        out_shape=(shape(5, 1024), shape(5, 256), shape(5, 256), shape(5, 1024),
+                   shape(5, 2048), shape(5, 2048), shape(5, 2048), shape(8, 128)),
+        in_specs=[hbm] * 4 + [vm] * 2,
+        out_specs=(vm,) * 8,
+        scratch_shapes=scratch
+        + [
+            pltpu.VMEM((16, 32, 128), BF),
+            pltpu.VMEM((16, 32, 128), BF),
+            pltpu.SemaphoreType.DMA((copies,)),
+            pltpu.SemaphoreType.DMA((copies,)),
+            pltpu.SemaphoreType.DMA((64,)),
+        ],
+        compiler_params=pltpu.CompilerParams(
+            collective_id=1, has_side_effects=True, vmem_limit_bytes=56 << 20
+        ),
+    )(qo, g, u, d, kv, gain_lines)
+
 
 norm_eps = 1e-06
 rope_base = 1000000.0
@@ -250,34 +852,6 @@
     return (grad_inputs, saved, width_gains, head_gains)
 
 
-def make_rows(saved, width_gains):
-    (
-        h_first,
-        grad_qraw,
-        grad_kraw,
-        grad_values,
-        context,
-        grad_attn,
-        h_second,
-        grad_gate,
-        grad_up,
-        hidden,
-        grad_mixed,
-    ) = saved
-    gain_cols = jnp.stack([item for item in width_gains], axis=1)
-    pieces = [
-        jnp.einsum("td,tq->dq", h_first, grad_qraw, preferred_element_type=jnp.float32),
-        jnp.einsum("td,tq->dq", h_first, grad_kraw, preferred_element_type=jnp.float32),
-        jnp.einsum("td,tq->dq", h_first, grad_values, preferred_element_type=jnp.float32),
-        jnp.einsum("td,tq->dq", grad_attn, context, preferred_element_type=jnp.float32),
-        jnp.einsum("td,tq->dq", h_second, grad_gate, preferred_element_type=jnp.float32),
-        jnp.einsum("td,tq->dq", h_second, grad_up, preferred_element_type=jnp.float32),
-        jnp.einsum("td,tq->dq", grad_mixed, hidden, preferred_element_type=jnp.float32),
-        gain_cols,
-    ]
-    return jnp.concatenate(pieces, axis=1)
-
-
 def per_device(
     tokens,
     segment_ids,
@@ -296,111 +870,55 @@
     pre_ffn_gain,
     post_ffn_gain,
 ):
-    micro_count = segment_ids.shape[0]
-    row_count = segment_ids.shape[1]
+    micro_count, row_count = segment_ids.shape
     feat_width = tokens.shape[1]
-    inputs = tokens.astype(jnp.float32).reshape(micro_count, row_count, feat_width)
-    upstream = cotangent.astype(jnp.float32).reshape(micro_count, row_count, feat_width)
-    held_weights = (
-        lax.all_gather(query_weight, "dp", axis=0, tiled=True),
-        lax.all_gather(key_weight, "dp", axis=0, tiled=True),
-        lax.all_gather(value_weight, "dp", axis=0, tiled=True),
-        lax.all_gather(out_weight, "dp", axis=1, tiled=True),
-        lax.all_gather(gate_weight, "dp", axis=0, tiled=True),
-        lax.all_gather(up_weight, "dp", axis=0, tiled=True),
-        lax.all_gather(down_weight, "dp", axis=1, tiled=True),
-        lax.all_gather(input_gain, "dp", axis=0, tiled=True),
-        lax.all_gather(query_gain, "dp", axis=0, tiled=True),
-        lax.all_gather(key_gain, "dp", axis=0, tiled=True),
-        lax.all_gather(post_attn_gain, "dp", axis=0, tiled=True),
-        lax.all_gather(pre_ffn_gain, "dp", axis=0, tiled=True),
-        lax.all_gather(post_ffn_gain, "dp", axis=0, tiled=True),
-    )
-    results = []
-    records = []
-    for micro_index in range(micro_count):
-        params = held_weights
-        result, record = forward_micro(params, inputs[micro_index], segment_ids[micro_index])
-        results.append(result.astype(jnp.bfloat16))
-        records.append(record)
-    held_weights = (
-        lax.all_gather(query_weight, "dp", axis=0, tiled=True),
-        lax.all_gather(key_weight, "dp", axis=0, tiled=True),
-        lax.all_gather(value_weight, "dp", axis=0, tiled=True),
-        lax.all_gather(out_weight, "dp", axis=1, tiled=True),
-        lax.all_gather(gate_weight, "dp", axis=0, tiled=True),
-        lax.all_gather(up_weight, "dp", axis=0, tiled=True),
-        lax.all_gather(down_weight, "dp", axis=1, tiled=True),
-        lax.all_gather(input_gain, "dp", axis=0, tiled=True),
-        lax.all_gather(query_gain, "dp", axis=0, tiled=True),
-        lax.all_gather(key_gain, "dp", axis=0, tiled=True),
-        lax.all_gather(post_attn_gain, "dp", axis=0, tiled=True),
-        lax.all_gather(pre_ffn_gain, "dp", axis=0, tiled=True),
-        lax.all_gather(post_ffn_gain, "dp", axis=0, tiled=True),
-    )
-    grad_list = []
-    saved_list = []
-    width_sum = None
-    head_sum = None
-    grad_share = None
-    for micro_index in range(micro_count):
-        params = held_weights
+    inputs = tokens.astype(F32).reshape(micro_count, row_count, feat_width)
+    upstream = cotangent.astype(F32).reshape(micro_count, row_count, feat_width)
+    gains = (input_gain, post_attn_gain, pre_ffn_gain, post_ffn_gain, query_gain, key_gain)
+    gain_rows = jnp.stack([jnp.pad(item.astype(F32), (0, 128 - item.shape[0])) for item in gains])
+    gain_rows = jnp.pad(gain_rows, ((0, 2), (0, 0)))
+    qo, gw, uw, dw, kv, lines = gather_weights(
+        query_weight, key_weight, value_weight, out_weight.T, gate_weight, up_weight, down_weight.T, gain_rows
+    )
+    qo, gw, uw, dw = (item.reshape(640, 2048) for item in (qo, gw, uw, dw))
+    params = (
+        qo[:, :1024], kv[:, :256], kv[:, 256:], qo[:, 1024:].T, gw, uw, dw.T,
+        lines[0], lines[4, :256], lines[5, :256], lines[1], lines[2], lines[3],
+    )
+    results, grad_list, saved_list, width_list, head_list = [], [], [], [], []
+    for micro in range(micro_count):
+        result, record = forward_micro(params, inputs[micro], segment_ids[micro])
         grad_inputs, saved, width_gains, head_gains = backward_micro(
-            params, inputs[micro_index], records[micro_index], upstream[micro_index]
+            params, inputs[micro], record, upstream[micro]
         )
+        results.append(result.astype(BF))
         grad_list.append(grad_inputs)
         saved_list.append(saved)
-        if width_sum is None:
-            width_sum = width_gains
-            head_sum = head_gains
-        else:
-            width_sum = tuple((left + right for left, right in zip(width_sum, width_gains)))
-            head_sum = tuple((left + right for left, right in zip(head_sum, head_gains)))
-    joined = tuple(
-        (jnp.concatenate([saved[field] for saved in saved_list], axis=0) for field in range(11))
-    )
-    grad_share = lax.psum_scatter(
-        make_rows(joined, width_sum), "dp", scatter_dimension=0, tiled=True
-    )
-    query_width = query_weight.shape[1]
-    head_dim = key_weight.shape[1]
-    hidden_width = gate_weight.shape[1]
-    edges = [
-        0,
-        query_width,
-        head_dim,
-        head_dim,
-        query_width,
-        hidden_width,
-        hidden_width,
-        hidden_width,
-        4,
-    ]
-    bounds = [sum(edges[: place + 1]) for place in range(len(edges))]
-    parts = [grad_share[:, bounds[place] : bounds[place + 1]] for place in range(8)]
-    grad_query_gain, grad_key_gain = (
-        lax.psum_scatter(head_sum[0], "dp", scatter_dimension=0, tiled=True),
-        lax.psum_scatter(head_sum[1], "dp", scatter_dimension=0, tiled=True),
-    )
-    gain_part = parts[7]
-    layer_out = jnp.concatenate(results, axis=0)
-    grad_tokens = jnp.concatenate(grad_list, axis=0)
+        width_list.append(width_gains)
+        head_list.append(head_gains)
+    (
+        h_first, grad_qraw, grad_kraw, grad_values, context, grad_attn,
+        h_second, grad_gate, grad_up, hidden, grad_mixed,
+    ) = (jnp.concatenate([saved[field] for saved in saved_list], axis=0) for field in range(11))
+
+    def outer(left, right):
+        return jnp.einsum("td,tq->dq", left, right, preferred_element_type=F32).astype(BF)
+
+    qo_grad = jnp.concatenate([outer(h_first, grad_qraw), outer(grad_attn, context)], axis=1)
+    kv_grad = outer(h_first, jnp.concatenate([grad_kraw, grad_values], axis=1))
+    grads = (qo_grad, outer(h_second, grad_gate), outer(h_second, grad_up), outer(grad_mixed, hidden))
+    width_sum = [sum(parts) for parts in zip(*width_list)]
+    head_sum = [jnp.pad(sum(parts), (0, 640 - 256)) for parts in zip(*head_list)]
+    grad_lines = jnp.pad(jnp.stack(width_sum + head_sum), ((0, 2), (0, 0)))
+    qg, kg, vg, og, gg, ug, dg, gain_grads = scatter_gradients(
+        *(item.reshape(4, 2, 80, 2048) for item in grads), kv_grad, grad_lines
+    )
     return (
-        layer_out,
-        grad_tokens,
-        parts[0],
-        parts[1],
-        parts[2],
-        parts[3].T,
-        parts[4],
-        parts[5],
-        parts[6].T,
-        gain_part[:, 0],
-        grad_query_gain,
-        grad_key_gain,
-        gain_part[:, 1],
-        gain_part[:, 2],
-        gain_part[:, 3],
+        jnp.concatenate(results, axis=0),
+        jnp.concatenate(grad_list, axis=0),
+        qg, kg, vg, og.T, gg, ug, dg.T,
+        gain_grads[0, :5], gain_grads[4, :2], gain_grads[5, :2],
+        gain_grads[1, :5], gain_grads[2, :5], gain_grads[3, :5],
     )
 
 

time: 663 us -> 177 us (0.27)
  waiting for transfers between devices: 316 us -> 0 us
  blocking collectives: 201 us -> 0 us
  Pallas kernels: 0 us -> 101 us
  local copies, waits for them, and re-layouts: 70.5 us -> 26.6 us
  between operations: 16.4 us -> 2.43 us
  matrix products: 42 us -> 34 us
    unnamed x7 -> x0, waiting for transfers between devices: 161 us -> none
    all_gather x5 -> x0, waiting for transfers between devices: 155 us -> none  [the longest x1 63.2 us: per_device(): lax.all_gather(up_weight, 'dp', axis=0, tiled=True)]
    unnamed x2 -> x0, blocking collectives: 132 us -> none
    pallas_call x0 -> x2, Pallas kernels: none -> 101 us  [the longest x1 51.8 us: gather_weights(): pl.pallas_call(gather_kernel, out_shape=(wide, wide, wide, wide, jax.Shap...]
    all_gather x2 -> x0, blocking collectives: 68.6 us -> none  [the longest x1 34.5 us: per_device(): lax.all_gather(value_weight, 'dp', axis=0, tiled=True)]
    concatenate x1 -> x0, local copies, waits for them, and re-layouts: 26.1 us -> none  [make_rows(): return jnp.concatenate(pieces, axis=1)]
    unnamed x293 -> x187, local copies, waits for them, and re-layouts: 33 us -> 14.5 us
    dot_general x7 -> x6, matrix products: 14.9 us -> 9.82 us  [outer(): jnp.einsum('td,tq->dq', left, right, preferred_element_type=F32).astype(BF)]
  transfers between devices with their start and end apart: 6 -> 0, of which waited for: 4 -> 0; matrix products, arithmetic and copies ran while one was open for 7% -> 0% of each run, Pallas kernels for 0% -> 0%
where the time goes in v1:
time: 177 us; the launch traced here: 176 us
  Pallas kernels  101 us (57%)
  matrix products  34 us (19%)
  local copies, waits for them, and re-layouts  26.6 us (15%)
  other arithmetic  12.2 us (7%)
  between operations  2.43 us (1%)
    pallas_call x1, Pallas kernels, gather_weights(): pl.pallas_call(gather_kernel, out_shape=(wide, wide, wide, wide, jax.Shap...  51.8 us
    pallas_call x1, Pallas kernels, scatter_gradients(): pl.pallas_call(scatter_kernel, out_shape=(shape(5, 1024), shape(5, 256),...  49.3 us
    unnamed x187, local copies, waits for them, and re-layouts  14.5 us
    dot_general x14, matrix products, product(): return jnp.dot(left, right, preferred_element_type=jnp.float32)  12.4 us
    dot_general x6, matrix products, outer(): jnp.einsum('td,tq->dq', left, right, preferred_element_type=F32).astype(BF)  9.82 us

profile of v1, /device:TPU:1, one launch (start us, length us, event | category | flops | bytes accessed | tf_op | source)
XLA Modules:
  0.0 176.3 jit_solution(15262623061025676361)
XLA Ops:
  0.7 0.8 slice_bitcast_fusion.7
  1.6 0.7 pad_bitcast_fusion.4
  2.3 0.7 pad_bitcast_fusion
  2.9 0.7 pad_bitcast_fusion.2
  4.2 0.7 compare_and_fusion.1
  4.9 1.0 convert_element_type.193
  6.1 1.0 convert_element_type.216
  7.1 51.8 %shard_map.271 = (bf16[4,2,80,2048]{3,2,1,0:T(8,128)(2,1)}, bf16[4,2,80,2048]{3,2,1,0:T(8,128)(2,1)}, bf16[4,2,80,2048]{3,2,1,0:T(8,128)(2,1)}, bf16[4,2,80,2048...) custom-call(bf16[5,1024]{1,0:T(8,128)(2,1)} %q.1, bf16[5,256]{1,0:T(8,128)(2,1)} %k.1, ...), custom_call_target="tpu_custom_call" | custom-call | tf_op jit(solution)/shard_map/pallas_call | solution.py:447
  58.9 1.4 fusion.180
  60.4 0.9 slice_reduce_fusion
  61.4 1.2 fusion.8
  62.6 1.8 %fusion.9 = bf16[96,256,1]{1,0,2:T(8,128)(2,1)} fusion(bf16[96,640]{1,0:T(8,128)(2,1)S(1)} %get-tuple-element.97, bf16[640,512]{1,0:T(8,128)(2,1)} %get-tuple-element.30), kind=kOutput, calls=%fused_computation.42 | convolution fusion | flops 31481856 | bytes 499712 | tf_op jit(solution)/shard_map/dot_general | solution.py:668
  64.4 1.3 multiply_reduce_fusion.35
  65.7 1.3 multiply_reduce_fusion.34
  67.6 1.0 fusion.133
  71.7 0.8 copy-done.5
  76.5 1.1 copy-done
  77.7 0.8 multiply_convert_fusion.2
  78.4 1.0 copy-done.2
  79.4 1.0 multiply_reduce_fusion.20
  80.4 1.0 multiply_convert_fusion.3
  81.4 1.0 multiply_reduce_fusion.24
  83.5 1.1 multiply_convert_fusion
  84.7 1.1 multiply_convert_fusion.1
  85.8 0.8 pad_maximum_fusion.2
  86.6 0.9 fusion.185
  87.6 0.9 fusion.186
  88.5 0.9 convolution_add_fusion.4
  89.4 1.1 multiply_reduce_fusion.7
  100.8 0.8 pad_maximum_fusion.1
  101.6 0.7 stack.50
  102.3 0.6 pad.85.gain_lines
  103.0 1.2 convolution_convert_fusion.5.kv
  104.8 0.8 convolution_convert_fusion.3
  105.6 1.8 pad_maximum_fusion
  107.4 2.4 %convolution_convert_fusion.1 = bf16[640,2048]{1,0:T(8,128)(2,1)} fusion(bf16[96,2048]{1,0:T(8,128)(2,1)S(1)} %copy-done.11, bf16[96,2048]{1,0:T(8,128)(2,1)S(1)} %copy-done.9, bf16[96,640]{1,0:T(8,128)(2,1)S(1)} %get-tuple-element.129, bf16[96,640]{1,0:T(8,128)(2,1)S(1)} %get-tuple-element.128), kind=kOutput, calls=%fused_computation.1 | convolution fusion | flops 506691584 | bytes 3653632 | tf_op jit(solution)/shard_map/td,tq->dq/dot_general | solution.py:905
  109.8 2.4 %convolution_convert_fusion.2 = bf16[640,2048]{1,0:T(8,128)(2,1)} fusion(bf16[96,2048]{1,0:T(8,128)(2,1)S(1)} %get-tuple-element.86, bf16[96,2048]{1,0:T(8,128)(2,1)S(1)} %copy-done.7, bf16[96,640]{1,0:T(8,128)(2,1)S(1)} %get-tuple-element.129, bf16[96,640]{1,0:T(8,128)(2,1)S(1)} %get-tuple-element.128), kind=kOutput, calls=%fused_computation.2 | convolution fusion | flops 506691584 | bytes 3653632 | tf_op jit(solution)/shard_map/td,tq->dq/dot_general | solution.py:905
  112.2 2.5 %convolution_convert_fusion = bf16[640,2048]{1,0:T(8,128)(2,1)} fusion(bf16[96,2048]{1,0:T(8,128)(2,1)S(1)} %get-tuple-element.172, bf16[96,2048]{1,0:T(8,128)(2,1)S(1)} %get-tuple-element.168, bf16[96,640]{1,0:T(8,128)(2,1)S(1)} %copy-done.17, bf16[96,640]{1,0:T(8,128)(2,1)S(1)} %copy-done.15), kind=kOutput, calls=%fused_computation | convolution fusion | flops 506691584 | bytes 3653632 | tf_op jit(solution)/shard_map/td,tq->dq/dot_general | solution.py:905
  114.7 49.3 %shard_map.272 = (f32[5,1024]{1,0:T(8,128)}, f32[5,256]{1,0:T(8,128)}, f32[5,256]{1,0:T(8,128)}, f32[5,1024]{1,0:T(8,128)}, f32[5,2048]{1,0:T(8,128)}, /*index=5...) custom-call(bf16[4,2,80,2048]{3,2,1,0:T(8,128)(2,1)} %bitcast.205, bf16[4,2,80,2048]{3,2,1,0:T(8,128)(2,1)} %bitcast.203, ...), custom_call_target="tpu_custom_call" | custom-call | tf_op jit(solution)/shard_map/pallas_call | solution.py:590
  163.9 1.3 slice_bitcast_fusion.3
  165.2 1.4 slice_bitcast_fusion
  166.6 1.4 copy.177
  168.0 1.3 copy.178
  169.3 1.3 copy.179
  170.6 1.4 copy.180
  171.9 1.5 copy.181
  173.4 1.5 copy.182
  174.9 1.5 copy.183
  (283 shorter events, 19.4 us)
Async XLA Ops:
  0.7 66.9 %copy-start.76 = (f32[128]{0:T(128)}, f32[128]{0:T(128)S(1)}, u32[]{:S(2)}) copy-start(f32[128]{0:T(128)S(1)} %multiply_exponential_fusion) | copy-start | bytes 1540
  1.5 66.0 %copy-start.78 = (f32[96]{0:T(128)}, f32[96]{0:T(128)S(1)}, u32[]{:S(2)}) copy-start(f32[96]{0:T(128)S(1)} %convert_element_type.208) | copy-start | bytes 1156
  1.6 66.0 %copy-start.80 = (f32[96]{0:T(128)}, f32[96]{0:T(128)S(1)}, u32[]{:S(2)}) copy-start(f32[96]{0:T(128)S(1)} %convert_element_type.197) | copy-start | bytes 1156
  6.1 62.9 %copy-start.82 = (f32[96]{0:T(128)}, f32[96]{0:T(128)S(1)}, u32[]{:S(2)}) copy-start(f32[96]{0:T(128)S(1)} %get-tuple-element.67) | copy-start | bytes 1156
  6.1 62.9 %copy-start.84 = (f32[96]{0:T(128)}, f32[96]{0:T(128)S(1)}, u32[]{:S(2)}) copy-start(f32[96]{0:T(128)S(1)} %get-tuple-element.68) | copy-start | bytes 1156
  6.1 61.1 %copy-start.68 = (f32[96]{0:T(128)}, f32[96]{0:T(128)S(1)}, u32[]{:S(2)}) copy-start(f32[96]{0:T(128)S(1)} %get-tuple-element.188) | copy-start | bytes 1156
  6.1 61.1 %copy-start.70 = (f32[96]{0:T(128)}, f32[96]{0:T(128)S(1)}, u32[]{:S(2)}) copy-start(f32[96]{0:T(128)S(1)} %get-tuple-element.189) | copy-start | bytes 1156
  58.9 9.7 %copy-start.4 = (bf16[4,2,80,2048]{3,2,1,0:T(8,128)(2,1)S(1)}, bf16[4,2,80,2048]{3,2,1,0:T(8,128)(2,1)}, u32[]{:S(2)}) copy-start(bf16[4,2,80,2048]{3,2,1,0:T(8,128)(2,1)} %get-tuple-element.31) | copy-start | bytes 7864324
  60.4 6.8 %copy-start.63 = (f32[1,256]{1,0:T(1,128)}, f32[1,256]{1,0:T(1,128)S(1)}, u32[]{:S(2)}) copy-start(f32[1,256]{1,0:T(1,128)S(1)} %get-tuple-element.117) | copy-start | bytes 3076
  62.6 8.8 %copy-start.37 = (bf16[96,256,1]{1,0,2:T(8,128)(2,1)}, bf16[96,256,1]{1,0,2:T(8,128)(2,1)S(1)}, u32[]{:S(2)}) copy-start(bf16[96,256,1]{1,0,2:T(8,128)(2,1)S(1)} %fusion.8) | copy-start | bytes 147460
  65.7 3.7 %copy-start.86 = (f32[96]{0:T(128)}, f32[96]{0:T(128)S(1)}, u32[]{:S(2)}) copy-start(f32[96]{0:T(128)S(1)} %get-tuple-element.156) | copy-start | bytes 1156
  67.0 2.6 %copy-start.12 = (f32[96,256]{1,0:T(8,128)}, f32[96,256]{1,0:T(8,128)S(1)}, u32[]{:S(2)}) copy-start(f32[96,256]{1,0:T(8,128)S(1)} %get-tuple-element.159) | copy-start | bytes 294916
  68.5 2.5 %copy-start.49 = (bf16[96,128]{1,0:T(8,128)(2,1)}, bf16[96,128]{1,0:T(8,128)(2,1)S(1)}, u32[]{:S(2)}) copy-start(bf16[96,128]{1,0:T(8,128)(2,1)S(1)} %get-tuple-element.112) | copy-start | bytes 73732
  68.5 2.5 %copy-start.51 = (bf16[96,128]{1,0:T(8,128)(2,1)}, bf16[96,128]{1,0:T(8,128)(2,1)S(1)}, u32[]{:S(2)}) copy-start(bf16[96,128]{1,0:T(8,128)(2,1)S(1)} %get-tuple-element.113) | copy-start | bytes 73732
  68.5 4.5 %copy-start.22 = (f32[96,128]{1,0:T(8,128)}, f32[96,128]{1,0:T(8,128)S(1)}, u32[]{:S(2)}) copy-start(f32[96,128]{1,0:T(8,128)S(1)} %get-tuple-element.154) | copy-start | bytes 147460
  68.5 4.5 %copy-start.24 = (f32[96,128]{1,0:T(8,128)}, f32[96,128]{1,0:T(8,128)S(1)}, u32[]{:S(2)}) copy-start(f32[96,128]{1,0:T(8,128)S(1)} %get-tuple-element.155) | copy-start | bytes 147460
  84.7 3.8 %copy-start.10 = (bf16[96,2048]{1,0:T(8,128)(2,1)}, bf16[96,2048]{1,0:T(8,128)(2,1)S(1)}, u32[]{:S(2)}) copy-start(bf16[96,2048]{1,0:T(8,128)(2,1)S(1)} %get-tuple-element.85) | copy-start | bytes 1179652
  85.8 2.7 %copy-start.6 = (bf16[96,2048]{1,0:T(8,128)(2,1)}, bf16[96,2048]{1,0:T(8,128)(2,1)S(1)}, u32[]{:S(2)}) copy-start(bf16[96,2048]{1,0:T(8,128)(2,1)S(1)} %get-tuple-element.84) | copy-start | bytes 1179652
  85.8 3.6 %copy-start.8 = (bf16[96,2048]{1,0:T(8,128)(2,1)}, bf16[96,2048]{1,0:T(8,128)(2,1)S(1)}, u32[]{:S(2)}) copy-start(bf16[96,2048]{1,0:T(8,128)(2,1)S(1)} %get-tuple-element.83) | copy-start | bytes 1179652
  92.1 7.4 %copy-start.26 = (bf16[96,256]{1,0:T(8,128)(2,1)}, bf16[96,256]{1,0:T(8,128)(2,1)S(1)}, u32[]{:S(2)}) copy-start(bf16[96,256]{1,0:T(8,128)(2,1)S(1)} %fusion.6) | copy-start | bytes 147460
  92.7 3.0 %copy-start.23 = (f32[96,128]{1,0:T(8,128)S(1)}, f32[96,128]{1,0:T(8,128)}, u32[]{:S(2)}) copy-start(f32[96,128]{1,0:T(8,128)} %copy-done.22) | copy-start | bytes 147460
  92.7 3.0 %copy-start.25 = (f32[96,128]{1,0:T(8,128)S(1)}, f32[96,128]{1,0:T(8,128)}, u32[]{:S(2)}) copy-start(f32[96,128]{1,0:T(8,128)} %copy-done.24) | copy-start | bytes 147460
  93.1 2.7 %copy-start.50 = (bf16[96,128]{1,0:T(8,128)(2,1)S(1)}, bf16[96,128]{1,0:T(8,128)(2,1)}, u32[]{:S(2)}) copy-start(bf16[96,128]{1,0:T(8,128)(2,1)} %copy-done.49) | copy-start | bytes 73732
  93.2 2.7 %copy-start.52 = (bf16[96,128]{1,0:T(8,128)(2,1)S(1)}, bf16[96,128]{1,0:T(8,128)(2,1)}, u32[]{:S(2)}) copy-start(bf16[96,128]{1,0:T(8,128)(2,1)} %copy-done.51) | copy-start | bytes 73732
  93.4 5.8 %copy-start.39 = (bf16[96,256]{1,0:T(8,128)(2,1)}, bf16[96,256]{1,0:T(8,128)(2,1)S(1)}, u32[]{:S(2)}) copy-start(bf16[96,256]{1,0:T(8,128)(2,1)S(1)} %fusion.7) | copy-start | bytes 147460
  93.4 2.7 %copy-start.19 = (f32[96,128]{1,0:T(8,128)S(1)}, f32[96,128]{1,0:T(8,128)}, u32[]{:S(2)}) copy-start(f32[96,128]{1,0:T(8,128)} %copy-done.18) | copy-start | bytes 147460
  93.4 2.7 %copy-start.21 = (f32[96,128]{1,0:T(8,128)S(1)}, f32[96,128]{1,0:T(8,128)}, u32[]{:S(2)}) copy-start(f32[96,128]{1,0:T(8,128)} %copy-done.20) | copy-start | bytes 147460
  93.7 2.5 %copy-start.56 = (f32[96,4]{0,1:T(4,128)S(1)}, f32[96,4]{0,1:T(4,128)}, u32[]{:S(2)}) copy-start(f32[96,4]{0,1:T(4,128)} %copy-done.55) | copy-start | bytes 4612
  93.7 2.5 %copy-start.62 = (f32[1,256]{1,0:T(1,128)S(1)}, f32[1,256]{1,0:T(1,128)}, u32[]{:S(2)}) copy-start(f32[1,256]{1,0:T(1,128)} %get-tuple-element.116) | copy-start | bytes 3076
  94.9 3.8 %copy-start.41 = (bf16[96,256]{1,0:T(8,128)(2,1)}, bf16[96,256]{1,0:T(8,128)(2,1)S(1)}, u32[]{:S(2)}) copy-start(bf16[96,256]{1,0:T(8,128)(2,1)S(1)} %get-tuple-element.130) | copy-start | bytes 147460
  94.9 4.0 %copy-start.43 = (bf16[96,256]{1,0:T(8,128)(2,1)}, bf16[96,256]{1,0:T(8,128)(2,1)S(1)}, u32[]{:S(2)}) copy-start(bf16[96,256]{1,0:T(8,128)(2,1)S(1)} %get-tuple-element.131) | copy-start | bytes 147460
  97.0 3.7 %copy-start.32 = (bf16[4,12,8,256]{3,2,0,1:T(8,128)(2,1)}, bf16[4,12,8,256]{3,2,0,1:T(8,128)(2,1)S(1)}, u32[]{:S(2)}) copy-start(bf16[4,12,8,256]{3,2,0,1:T(8,128)(2,1)S(1)} %copy.136) | copy-start | bytes 589828
  97.6 3.2 %copy-start.34 = (bf16[4,12,8,256]{3,2,0,1:T(8,128)(2,1)}, bf16[4,12,8,256]{3,2,0,1:T(8,128)(2,1)S(1)}, u32[]{:S(2)}) copy-start(bf16[4,12,8,256]{3,2,0,1:T(8,128)(2,1)S(1)} %copy.137) | copy-start | bytes 589828
  98.1 2.4 %copy-start.83 = (f32[96]{0:T(128)S(1)}, f32[96]{0:T(128)}, u32[]{:S(2)}) copy-start(f32[96]{0:T(128)} %copy-done.82) | copy-start | bytes 1156
  99.2 2.4 %copy-start.67 = (f32[1,640]{1,0:T(1,128)S(1)}, f32[1,640]{1,0:T(1,128)}, u32[]{:S(2)}) copy-start(f32[1,640]{1,0:T(1,128)} %add.357) | copy-start | bytes 7684
  99.2 3.8 %copy-start.42 = (bf16[96,256]{1,0:T(8,128)(2,1)S(1)}, bf16[96,256]{1,0:T(8,128)(2,1)}, u32[]{:S(2)}) copy-start(bf16[96,256]{1,0:T(8,128)(2,1)} %copy-done.41) | copy-start | bytes 147460
  99.2 3.7 %copy-start.44 = (bf16[96,256]{1,0:T(8,128)(2,1)S(1)}, bf16[96,256]{1,0:T(8,128)(2,1)}, u32[]{:S(2)}) copy-start(bf16[96,256]{1,0:T(8,128)(2,1)} %copy-done.43) | copy-start | bytes 147460
  99.5 3.5 %copy-start.40 = (bf16[96,256]{1,0:T(8,128)(2,1)S(1)}, bf16[96,256]{1,0:T(8,128)(2,1)}, u32[]{:S(2)}) copy-start(bf16[96,256]{1,0:T(8,128)(2,1)} %copy-done.39) | copy-start | bytes 147460
  99.9 3.1 %copy-start.27 = (bf16[96,256]{1,0:T(8,128)(2,1)S(1)}, bf16[96,256]{1,0:T(8,128)(2,1)}, u32[]{:S(2)}) copy-start(bf16[96,256]{1,0:T(8,128)(2,1)} %copy-done.26) | copy-start | bytes 147460
  100.7 4.0 %copy-start.29 = (bf16[4,12,8,256]{3,2,0,1:T(8,128)(2,1)S(1)}, bf16[4,12,8,256]{3,2,0,1:T(8,128)(2,1)}, u32[]{:S(2)}) copy-start(bf16[4,12,8,256]{3,2,0,1:T(8,128)(2,1)} %copy-done.28) | copy-start | bytes 589828
  100.7 4.0 %copy-start.31 = (bf16[4,12,8,256]{3,2,0,1:T(8,128)(2,1)S(1)}, bf16[4,12,8,256]{3,2,0,1:T(8,128)(2,1)}, u32[]{:S(2)}) copy-start(bf16[4,12,8,256]{3,2,0,1:T(8,128)(2,1)} %copy-done.30) | copy-start | bytes 589828
  100.7 4.0 %copy-start.46 = (bf16[96,640]{1,0:T(8,128)(2,1)S(1)}, bf16[96,640]{1,0:T(8,128)(2,1)}, u32[]{:S(2)}) copy-start(bf16[96,640]{1,0:T(8,128)(2,1)} %copy-done.45) | copy-start | bytes 368644
  100.7 4.0 %copy-start.48 = (bf16[96,640]{1,0:T(8,128)(2,1)S(1)}, bf16[96,640]{1,0:T(8,128)(2,1)}, u32[]{:S(2)}) copy-start(bf16[96,640]{1,0:T(8,128)(2,1)} %copy-done.47) | copy-start | bytes 368644
  100.8 3.4 %copy-start.33 = (bf16[4,12,8,256]{3,2,0,1:T(8,128)(2,1)S(1)}, bf16[4,12,8,256]{3,2,0,1:T(8,128)(2,1)}, u32[]{:S(2)}) copy-start(bf16[4,12,8,256]{3,2,0,1:T(8,128)(2,1)} %copy-done.32) | copy-start | bytes 589828
  100.8 3.4 %copy-start.35 = (bf16[4,12,8,256]{3,2,0,1:T(8,128)(2,1)S(1)}, bf16[4,12,8,256]{3,2,0,1:T(8,128)(2,1)}, u32[]{:S(2)}) copy-start(bf16[4,12,8,256]{3,2,0,1:T(8,128)(2,1)} %copy-done.34) | copy-start | bytes 589828
  107.4 2.4 %copy-start.7 = (bf16[96,2048]{1,0:T(8,128)(2,1)S(1)}, bf16[96,2048]{1,0:T(8,128)(2,1)}, u32[]{:S(2)}) copy-start(bf16[96,2048]{1,0:T(8,128)(2,1)} %copy-done.6) | copy-start | bytes 1179652
  109.8 2.4 %copy-start.15 = (bf16[96,640]{1,0:T(8,128)(2,1)S(1)}, bf16[96,640]{1,0:T(8,128)(2,1)}, u32[]{:S(2)}) copy-start(bf16[96,640]{1,0:T(8,128)(2,1)} %copy-done.14) | copy-start | bytes 368644
  109.8 2.4 %copy-start.17 = (bf16[96,640]{1,0:T(8,128)(2,1)S(1)}, bf16[96,640]{1,0:T(8,128)(2,1)}, u32[]{:S(2)}) copy-start(bf16[96,640]{1,0:T(8,128)(2,1)} %copy-done.16) | copy-start | bytes 368644
  (42 other events, 72.7 us)

commit v2 on v1

v2 whole, which is shorter than its diff:
```python
import functools
import math

import jax
import jax.numpy as jnp
from jax import lax
from jax.experimental import pallas as pl
from jax.experimental.pallas import tpu as pltpu
from jax.sharding import PartitionSpec as P

BF = jnp.bfloat16
F32 = jnp.float32
MESH = pl.DeviceIdType.MESH


class Place:
    def __init__(self):
        me = lax.axis_index("dp")
        self.me = me
        self.c = lax.rem(me, 2)
        self.z = lax.rem(lax.div(me, 2), 4)
        self.y = lax.rem(lax.div(me, 8), 4)
        self.x = lax.div(me, 32)
        self.yl = lax.rem(self.y, 2)
        self.yh = lax.div(self.y, 2)
        self.at = {"x": self.x, "y": self.y, "z": self.z}

    def device(self, x, y, z, c):
        return ((x * 4 + y) * 4 + z) * 2 + c

    def moved(self, axis, by):
        return lax.rem(self.at[axis] + by, 4)

    def peer(self, axis, by):
        spot = dict(self.at)
        spot[axis] = self.moved(axis, by)
        return self.device(spot["x"], spot["y"], spot["z"], self.c)

    def sibling(self):
        return self.device(self.x, self.y, self.z, 1 - self.c)

    def group_peers(self):
        found = []
        for dyl in range(2):
            for dz in range(4):
                for dc in range(2):
                    if dyl or dz or dc:
                        yl = lax.rem(self.yl + dyl, 2)
                        z = lax.rem(self.z + dz, 4)
                        c = lax.rem(self.c + dc, 2)
                        found.append(
                            (
                                self.device(self.x, self.yh * 2 + yl, z, c),
                                c * 8 + yl * 4 + z,
                                yl * 8 + z * 2 + c,
                            )
                        )
        return found

    def slot(self):
        return self.c * 8 + self.yl * 4 + self.z

    def natural(self):
        return self.yl * 8 + self.z * 2 + self.c

    def greet(self):
        others = [item[0] for item in self.group_peers()]
        others += [self.peer("x", by) for by in (1, 2, 3)]
        others += [
            self.device(self.x, (1 - self.yh) * 2 + yl, self.z, self.c) for yl in range(2)
        ]
        barrier = pltpu.get_barrier_semaphore()
        for other in others:
            pl.semaphore_signal(barrier, inc=1, device_id=(other,), device_id_type=MESH)
        pl.semaphore_wait(barrier, len(others))


def region(select, half=None):
    index = []
    for axis in "xyz":
        value = select[axis]
        if value is None:
            cut = half is not None
            if axis == "y":
                index += [pl.ds(half, 1) if cut else slice(None), slice(None)]
            else:
                index.append(pl.ds(2 * half, 2) if cut else slice(None))
            half = None
        elif axis == "y":
            index += [lax.div(value, 2), lax.rem(value, 2)]
        else:
            index.append(value)
    return tuple(index)


def half_shape(whole):
    shape, cut = [], True
    for axis in "xyz":
        if axis in whole:
            if axis == "y":
                shape += [1 if cut else 2, 2]
            else:
                shape.append(2 if cut else 4)
            cut = False
    return tuple(shape)


def whole_shape(whole):
    shape = []
    for axis in "xyz":
        if axis in whole:
            shape += [2, 2] if axis == "y" else [4]
    return tuple(shape)


class Sender:
    def __init__(self, send_sems, recv_sems):
        self.send_sems, self.recv_sems = send_sems, recv_sems
        self.used = 0
        self.open = []

    def send(self, source, target, device):
        copy = pltpu.make_async_remote_copy(
            src_ref=source,
            dst_ref=target,
            send_sem=self.send_sems.at[self.used],
            recv_sem=self.recv_sems.at[self.used],
            device_id=(device,),
            device_id_type=MESH,
        )
        self.used += 1
        copy.start()
        self.open.append(copy)
        return copy

    def finish(self):
        for copy in self.open:
            copy.wait_send()
        self.open = []


def gather_class(place, sender, ref, rows, order):
    tail = (pl.ds(rows[0], rows[1]), slice(None))

    def view(select, half=None):
        return ref.at[(place.c,) + region(select, half) + tail]

    def select_for(step, value):
        chosen = {}
        for at, axis in enumerate(order):
            chosen[axis] = None if at < step else value if at == step else place.at[axis]
        return chosen

    def push(part, device):
        return sender.send(part, part, device)

    for step in (0, 1):
        axis = order[step]
        own = view(select_for(step, place.at[axis]))
        sent = [push(own, place.peer(axis, by)) for by in (1, 3, 2)]
        yield
        for copy in sent:
            copy.wait_recv()
    axis = order[2]
    right, left = place.peer(axis, 1), place.peer(axis, 3)
    mine = select_for(2, place.at[axis])
    of_right = select_for(2, place.moved(axis, 1))
    of_left = select_for(2, place.moved(axis, 3))
    of_far = select_for(2, place.moved(axis, 2))
    r0 = push(view(mine, 0), right)
    l1 = push(view(mine, 1), left)
    r1 = push(view(mine, 1), right)
    l0 = push(view(mine, 0), left)
    twin = [push(view(mine), place.sibling())]
    yield
    r0.wait_recv()
    f0 = push(view(of_left, 0), right)
    l1.wait_recv()
    f1 = push(view(of_right, 1), left)
    yield
    r1.wait_recv()
    twin.append(push(view(of_left), place.sibling()))
    l0.wait_recv()
    twin.append(push(view(of_right), place.sibling()))
    yield
    f0.wait_recv()
    twin.append(push(view(of_far, 0), place.sibling()))
    f1.wait_recv()
    twin.append(push(view(of_far, 1), place.sibling()))
    yield
    for copy in twin:
        copy.wait_recv()


GATHER_COPIES = 17
SCATTER_COPIES = 16


def scatter_class(place, sender, ref, twin_ref, landing, rows, order):
    tail = (pl.ds(rows[0], rows[1]), slice(None))
    order = order[::-1]

    def at(select, half=None):
        return (place.c,) + region(select, half) + tail

    def select_for(step, value):
        chosen = {}
        for where, axis in enumerate(order):
            chosen[axis] = (
                place.at[axis] if where < step else value if where == step else None
            )
        return chosen

    def add(index, *others):
        total = ref[index].astype(F32)
        for other in others:
            total = total + other.astype(F32)
        ref[index] = total.astype(BF)

    axis = order[0]
    pieces = []
    for by in (2, 1, 3, 0):
        part = region(select_for(0, place.moved(axis, by))) + tail
        pieces.append(
            (part, sender.send(ref.at[(1 - place.c,) + part], twin_ref.at[part], place.sibling()))
        )
    yield

    def joined(which):
        part, copy = pieces[which]
        copy.wait_recv()
        add((place.c,) + part, twin_ref[part])

    land = landing[0]
    right, left = place.peer(axis, 1), place.peer(axis, 3)
    mine = select_for(0, place.at[axis])
    to_right = select_for(0, place.moved(axis, 1))
    to_left = select_for(0, place.moved(axis, 3))
    far = select_for(0, place.moved(axis, 2))
    joined(0)
    f0 = sender.send(ref.at[at(far, 0)], land.at[0], right)
    f1 = sender.send(ref.at[at(far, 1)], land.at[1], left)
    joined(1)
    r1 = sender.send(ref.at[at(to_right, 1)], land.at[2], right)
    joined(2)
    l0 = sender.send(ref.at[at(to_left, 0)], land.at[3], left)
    joined(3)
    yield
    f0.wait_recv()
    add(at(to_right, 0), land[0])
    r0 = sender.send(ref.at[at(to_right, 0)], land.at[4], right)
    f1.wait_recv()
    add(at(to_left, 1), land[1])
    l1 = sender.send(ref.at[at(to_left, 1)], land.at[5], left)
    yield
    r1.wait_recv()
    l0.wait_recv()
    r0.wait_recv()
    l1.wait_recv()
    add(at(mine, 0), land[4], land[3])
    add(at(mine, 1), land[2], land[5])
    for step in (1, 2):
        axis = order[step]
        land = landing[step]
        sent = [
            sender.send(
                ref.at[at(select_for(step, place.moved(axis, by)))],
                land.at[by - 1],
                place.peer(axis, by),
            )
            for by in (1, 3, 2)
        ]
        yield
        for copy in sent:
            copy.wait_recv()
        add(at(select_for(step, place.at[axis])), land[0], land[1], land[2])


def landing_shapes(rows, order):
    back = order[::-1]
    return [
        pltpu.VMEM((6,) + half_shape(back[1:]) + (rows, 128), BF),
        pltpu.VMEM((3,) + whole_shape(back[2:]) + (rows, 128), BF),
        pltpu.VMEM((3, rows, 128), BF),
    ]


def picker(part, transposed=False):
    i = lax.broadcasted_iota(jnp.int32, (80, 512), 0)
    j = lax.broadcasted_iota(jnp.int32, (80, 512), 1)
    n = lax.shift_right_logical(j, 5)
    r = lax.bitwise_and(j, 7)
    m = lax.bitwise_and(lax.shift_right_logical(j, 3), 3)
    hit = (m == part) & (r < 5) & (i == n * 5 + r)
    return jnp.where(hit, 1.0, 0.0).astype(BF)


def stacked(parts):
    pad = jnp.zeros((3, 128), F32)
    return jnp.concatenate(
        [item for part in parts for item in (part.astype(F32), pad)], axis=0
    )


CLASSES = (
    (0, 0, 32, "xyz"),
    (0, 32, 48, "yzx"),
    (4, 0, 32, "zxy"),
    (1, 0, 80, "xyz"),
    (2, 0, 80, "yzx"),
    (3, 0, 80, "zxy"),
)
BLOCK_ROWS = (80, 80, 80, 80, 32)


def fill_messages(q, o, k, v, g, u, d, gains, msgs, kv_block):
    for slot in range(16):
        lanes = slice(slot * 128, slot * 128 + 128)
        narrow = slice(slot % 8 * 128, slot % 8 * 128 + 128)
        qo = q[:, narrow] if slot < 8 else o[:, narrow]
        msgs[slot] = stacked([g[:, lanes], u[:, lanes], d[:, lanes], qo]).astype(BF)
    flat = stacked([k[:, 0:128], k[:, 128:256], v[:, 0:128], v[:, 128:256]])
    row = lax.broadcasted_iota(jnp.int32, (32, 128), 0)
    for at, target in enumerate(GAIN_ROWS):
        flat = jnp.where(row == target, gains[at : at + 1, :], flat)
    kv_block[...] = flat.astype(BF)


GAIN_ROWS = (5, 13, 21, 29, 6, 14)


def spread_rows(buf, row):
    takes = []
    for x in range(4):
        for yh in range(2):
            for yl in range(2):
                both = [
                    jnp.concatenate(
                        [buf[c, x, yh, yl, z, row // 8 * 8 : row // 8 * 8 + 8, :] for c in range(2)], 0
                    )
                    for z in range(4)
                ]
                takes += both
    every = jnp.concatenate(takes, axis=0)
    i = lax.broadcasted_iota(jnp.int32, (128, 1024), 0)
    j = lax.broadcasted_iota(jnp.int32, (128, 1024), 1)
    pick = jnp.where(j == i * 8 + row % 8, 1.0, 0.0).astype(BF)
    return jnp.dot(pick, every, preferred_element_type=F32)


def gain_line(buf, row, each, width):
    held = spread_rows(buf, row)
    count = lax.broadcasted_iota(jnp.int32, (128, width), 0)
    lane = lax.broadcasted_iota(jnp.int32, (128, width), 1)
    place_in = lane - count * each
    r = lax.broadcasted_iota(jnp.int32, (128, width), 0)
    rep = jnp.where(lax.rem(lane, each) == r, 1.0, 0.0).astype(BF)
    lined = jnp.dot(held.astype(BF), rep, preferred_element_type=F32)
    lined = jnp.where((place_in >= 0) & (place_in < each), lined, 0.0)
    return jnp.sum(lined, axis=0, keepdims=True)


def exchange_start(place, sender, msgs, recv):
    return [
        sender.send(msgs.at[slot], recv.at[place.natural()], device)
        for device, slot, _ in place.group_peers()
    ]


def exchange_take(place, copies, msgs, recv, bufs, kv_block):
    recv[place.natural()] = msgs[place.slot()]
    spot = (place.c, place.x, place.yh, place.yl, place.z)
    bufs[4][spot] = kv_block[...]
    for copy in copies:
        copy.wait_recv()
    flat = recv[...].reshape(512, 128)
    for part, buf in ((3, bufs[0]), (0, bufs[1]), (1, bufs[2]), (2, bufs[3])):
        buf[spot] = jnp.dot(picker(part), flat, preferred_element_type=F32).astype(BF)


def spread_gain(line, each):
    width = line.shape[1]
    count = lax.broadcasted_iota(jnp.int32, (128, width), 0)
    lane = lax.broadcasted_iota(jnp.int32, (128, width), 1)
    inside = lane - count * each
    kept = jnp.where((inside >= 0) & (inside < each), jnp.broadcast_to(line, (128, width)), 0.0)
    r = lax.broadcasted_iota(jnp.int32, (width, 128), 0)
    to = lax.broadcasted_iota(jnp.int32, (width, 128), 1)
    pick = jnp.where(lax.rem(r, each) == to, 1.0, 0.0).astype(BF)
    return jnp.dot(kept.astype(BF), pick, preferred_element_type=F32)


def fill_kv_gradient(kv, gain_lines, buf):
    gains = [spread_gain(line, 5 if at < 4 else 2) for at, line in enumerate(gain_lines)]
    row = lax.broadcasted_iota(jnp.int32, (512, 128), 0)
    seat = lax.bitwise_and(row, 31)
    n = lax.broadcasted_iota(jnp.int32, (512, 16), 0)
    m = lax.broadcasted_iota(jnp.int32, (512, 16), 1)
    repeat = jnp.where(lax.shift_right_logical(n, 5) == m, 1.0, 0.0).astype(BF)
    for group in range(8):
        flat = jnp.zeros((512, 128), F32)
        for part in range(4):
            flat = flat + lax.dot_general(
                picker(part), kv(group, part), (((0,), (0,)), ((), ())), preferred_element_type=F32
            )
        for at, target in enumerate(GAIN_ROWS):
            own = gains[at][group * 16 : group * 16 + 16].astype(BF)
            flat = jnp.where(
                seat == target, jnp.dot(repeat, own, preferred_element_type=F32), flat
            )
        flat = flat.astype(BF)
        for n16 in range(16):
            yl, z, c = n16 // 8, n16 // 2 % 4, n16 % 2
            buf[c, group // 2, group % 2, yl, z] = flat[n16 * 32 : n16 * 32 + 32]


def exchange_out(place, sender, msgs, recv, bufs):
    spot = (place.c, place.x, place.yh, place.yl, place.z)
    flat = jnp.zeros((512, 128), F32)
    for part, buf in ((3, bufs[0]), (0, bufs[1]), (1, bufs[2]), (2, bufs[3])):
        flat = flat + lax.dot_general(
            picker(part), buf[spot], (((0,), (0,)), ((), ())), preferred_element_type=F32
        )
    msgs[...] = flat.astype(BF).reshape(16, 32, 128)
    copies = [
        sender.send(msgs.at[natural], recv.at[place.slot()], device)
        for device, _, natural in place.group_peers()
    ]
    recv[place.slot()] = msgs[place.natural()]
    for copy in copies:
        copy.wait_recv()


NORM_EPS = 1e-06
ROPE_BASE = 1000000.0
MASKED = -1e30
ROWS = 96
PACKS = 2
HEADS = 4


def matmul(left, right):
    return jnp.dot(left, right, preferred_element_type=F32)


def matmul_t(left, right):
    return lax.dot_general(left, right, (((1,), (1,)), ((), ())), preferred_element_type=F32)


def t_matmul(left, right):
    return lax.dot_general(left, right, (((0,), (0,)), ((), ())), preferred_element_type=F32)


def inverse_rms(v):
    return lax.rsqrt(jnp.mean(v * v, axis=-1, keepdims=True) + NORM_EPS)


def rms_back(v, gain, dy):
    r = inverse_rms(v)
    n = v * r
    dg = dy * gain
    dv = r * (dg - n * jnp.mean(dg * n, axis=-1, keepdims=True))
    return dv, jnp.sum(dy * n, axis=0, keepdims=True)


def turn(v, cosine, sine):
    first, second = v[:, 0:128], v[:, 128:256]
    return jnp.concatenate(
        [first * cosine - second * sine, second * cosine + first * sine], axis=1
    )


def spot_of(t):
    return lax.div(t, 4), lax.rem(lax.div(t, 2), 2), lax.rem(t, 2) * 2


def read_tile(buf, t):
    c, yl, z = spot_of(t)
    return jnp.concatenate(
        [buf[c, :, :, yl, z + k].reshape(640, 128) for k in range(2)], axis=1
    )


def write_tile(buf, t, value):
    c, yl, z = spot_of(t)
    value = value.astype(BF)
    for k in range(2):
        buf[c, :, :, yl, z + k] = value[:, k * 128 : k * 128 + 128].reshape(4, 2, 80, 128)


def read_kv(buf, scratch):
    def group(g, carry):
        x, yh = lax.div(g, 2), lax.rem(g, 2)
        blocks = [buf[c, x, yh, yl, z] for yl in range(2) for z in range(4) for c in range(2)]
        flat = jnp.concatenate(blocks, axis=0)
        rows = pl.ds(pl.multiple_of(g * 80, 16), 80)
        for part in range(4):
            scratch[rows, part * 128 : part * 128 + 128] = matmul(picker(part), flat).astype(BF)
        return carry

    lax.fori_loop(0, 8, group, 0)


def tick(tasks):
    for task in list(tasks):
        try:
            next(task)
        except StopIteration:
            tasks.remove(task)


def drain(tasks):
    while tasks:
        tick(tasks)


def layer_kernel(
    tokens, segments, cotangent, q, k, v, o, g, u, d, gains,
    layer_out, grad_tokens, part_out, kv_out,
    *scratch,
):
    weights, grads, twins = scratch[0:5], scratch[5:10], scratch[10:15]
    scratch = scratch[15:]
    landings, scratch = scratch[: 3 * len(CLASSES)], scratch[3 * len(CLASSES) :]
    (
        msgs, recv, msgs_back, recv_back, kv_block, kv_weight, lines,
        h1_s, qraw_s, kraw_s, qf_s, kf_s, vb_s, prob_s, ctx_s, attn_s, x1_s, h2_s,
        slope_s, gelu_s, hidden_s, mixed_s, dm_s, dh2_s, dx1_s, da_s, dctx_s, dq_s, dkv_s,
        cos_s, sin_s, h2t_s, dmt_s,
        send_sems, recv_sems,
    ) = scratch
    place = Place()
    fill_messages(q, o, k, v, g, u, d, gains, msgs, kv_block)
    place.greet()
    sender = Sender(send_sems, recv_sems)
    arrivals = exchange_start(place, sender, msgs, recv)

    t_of = lax.broadcasted_iota(jnp.int32, (ROWS, ROWS), 0)
    u_of = lax.broadcasted_iota(jnp.int32, (ROWS, ROWS), 1)
    lane = lax.broadcasted_iota(jnp.int32, (1, 128), 1).astype(F32)
    frequency = jnp.exp(-math.log(ROPE_BASE) * 2.0 * lane / 256.0)
    allowed = []
    for b in range(PACKS):
        row = jnp.broadcast_to(segments[b : b + 1, :].astype(F32), (ROWS, ROWS))
        same = row == row.T
        earlier = jnp.where(same & (u_of < t_of), 1.0, 0.0)
        angles = jnp.sum(earlier, axis=1, keepdims=True) * frequency
        cos_s[b * ROWS : b * ROWS + ROWS] = jnp.cos(angles)
        sin_s[b * ROWS : b * ROWS + ROWS] = jnp.sin(angles)
        allowed.append(same & (u_of <= t_of))

    exchange_take(place, arrivals, msgs, recv, weights, kv_block)

    def gather(at):
        which, first, count, order = CLASSES[at]
        return gather_class(place, sender, weights[which], (first, count), order)

    near, wide = [gather(at) for at in range(3)], [gather(at) for at in range(3, 6)]
    while near:
        tick(near)
        tick(wide)

    read_kv(weights[4], kv_weight)
    lines[...] = jnp.zeros((8, 640), F32)
    for at, row in enumerate(GAIN_ROWS):
        if at < 4:
            lines[at : at + 1, :] = gain_line(weights[4], row, 5, 640)
        else:
            lines[at : at + 1, 0:256] = gain_line(weights[4], row, 2, 256)
    input_gain, post_attn_gain = lines[0:1, :], lines[1:2, :]
    pre_ffn_gain, post_ffn_gain = lines[2:3, :], lines[3:4, :]
    query_gain, key_gain = lines[4:5, 0:256], lines[5:6, 0:256]
    tick(wide)

    x = tokens[...].astype(F32)
    h1_s[...] = (x * inverse_rms(x) * input_gain).astype(BF)
    cosine, sine = cos_s[...], sin_s[...]
    h1 = h1_s[...]
    for h in range(HEADS):
        raw = matmul(h1, read_tile(weights[0], h))
        qraw_s[h] = raw
        query = turn(raw * inverse_rms(raw) * query_gain, cosine, sine) * (1.0 / 16.0)
        for b in range(PACKS):
            qf_s[b, h * ROWS : h * ROWS + ROWS] = query[b * ROWS : b * ROWS + ROWS].astype(BF)
    tick(wide)
    raw = matmul(h1, kv_weight[:, 0:256])
    kraw_s[...] = raw
    kf_s[...] = turn(raw * inverse_rms(raw) * key_gain, cosine, sine).astype(BF)
    vb_s[...] = matmul(h1, kv_weight[:, 256:512]).astype(BF)
    for b in range(PACKS):
        mine = slice(b * ROWS, b * ROWS + ROWS)
        scores = matmul_t(qf_s[b], kf_s[mine])
        scores = jnp.where(jnp.concatenate([allowed[b]] * HEADS, axis=0), scores, MASKED)
        grown = jnp.exp(scores - jnp.max(scores, axis=-1, keepdims=True))
        prob = grown / jnp.sum(grown, axis=-1, keepdims=True)
        prob_s[b] = prob
        context = matmul(prob.astype(BF), vb_s[mine]).astype(BF)
        for h in range(HEADS):
            ctx_s[h, mine] = context[h * ROWS : h * ROWS + ROWS]
    tick(wide)
    attn = matmul_t(ctx_s[0], read_tile(weights[0], 4))
    for h in range(1, HEADS):
        attn = attn + matmul_t(ctx_s[h], read_tile(weights[0], 4 + h))
    attn_s[...] = attn
    x1 = x + attn * inverse_rms(attn) * post_attn_gain
    x1_s[...] = x1
    h2_s[...] = (x1 * inverse_rms(x1) * pre_ffn_gain).astype(BF)
    h2t_s[...] = h2_s[...].astype(F32).T.astype(BF)
    tick(wide)
    drain(wide)

    mixed_s[...] = jnp.zeros((PACKS * ROWS, 640), F32)

    def feed(t, carry):
        h2 = h2_s[...]
        gate = matmul(h2, read_tile(weights[1], t))
        up = matmul(h2, read_tile(weights[2], t))
        rate = math.sqrt(2.0 / math.pi)
        square = gate * gate
        bent = jnp.tanh(rate * gate * (1.0 + 0.044715 * square))
        half = 0.5 * (1.0 + bent)
        gelu = gate * half
        slope = half + 0.5 * gate * (1.0 - bent * bent) * rate * (1.0 + 3 * 0.044715 * square)
        gelu_s[t] = gelu
        slope_s[t] = up * slope
        hidden = (gelu * up).astype(BF)
        hidden_s[t] = hidden
        mixed_s[...] += matmul_t(hidden, read_tile(weights[3], t))
        return carry

    lax.fori_loop(0, 8, feed, 0)

    c = cotangent[...].astype(F32)
    mixed = mixed_s[...]
    layer_out[...] = (x1_s[...] + mixed * inverse_rms(mixed) * post_ffn_gain).astype(BF)
    dm, post_ffn_line = rms_back(mixed, post_ffn_gain, c)
    dm_s[...] = dm.astype(BF)
    dmt_s[...] = dm_s[...].astype(F32).T.astype(BF)
    dh2_s[...] = jnp.zeros((PACKS * ROWS, 640), F32)

    def feed_back(t):
        dh = matmul(dm_s[...], read_tile(weights[3], t))
        dgate = (dh * slope_s[t]).astype(BF)
        dup = (dh * gelu_s[t]).astype(BF)
        dh2_s[...] += matmul_t(dgate, read_tile(weights[1], t)) + matmul_t(
            dup, read_tile(weights[2], t)
        )
        write_tile(grads[3], t, matmul(dmt_s[...], hidden_s[t]))
        write_tile(grads[1], t, matmul(h2t_s[...], dgate))
        write_tile(grads[2], t, matmul(h2t_s[...], dup))

    def first_half(i, carry):
        feed_back((1 - place.c) * 4 + i)
        return carry

    def second_half(i, carry):
        feed_back(place.c * 4 + i)
        return carry

    def scatter(at):
        which, first, count, order = CLASSES[at]
        return scatter_class(
            place, sender, grads[which], twins[which], landings[3 * at : 3 * at + 3],
            (first, count), order,
        )

    lax.fori_loop(0, 4, first_half, 0)
    wide = [scatter(at) for at in range(3, 6)]
    tick(wide)
    lax.fori_loop(0, 4, second_half, 0)
    tick(wide)

    dx1_part, pre_ffn_line = rms_back(x1_s[...], pre_ffn_gain, dh2_s[...])
    dx1 = c + dx1_part
    dx1_s[...] = dx1
    da, post_attn_line = rms_back(attn_s[...], post_attn_gain, dx1)
    da_s[...] = da.astype(BF)
    dat = da_s[...].astype(F32).T.astype(BF)
    tick(wide)
    for h in range(HEADS):
        dctx = matmul(da_s[...], read_tile(weights[0], 4 + h)).astype(BF)
        for b in range(PACKS):
            dctx_s[b, h * ROWS : h * ROWS + ROWS] = dctx[b * ROWS : b * ROWS + ROWS]
        write_tile(grads[0], 4 + h, matmul(dat, ctx_s[h]))
    tick(wide)
    query_line = jnp.zeros((1, 256), F32)
    key_line = jnp.zeros((1, 256), F32)
    for b in range(PACKS):
        mine = slice(b * ROWS, b * ROWS + ROWS)
        prob, dctx = prob_s[b], dctx_s[b]
        dp = matmul_t(dctx, vb_s[mine])
        ds = (prob * (dp - jnp.sum(prob * dp, axis=-1, keepdims=True))).astype(BF)
        dkv_s[mine, 256:512] = t_matmul(prob.astype(BF), dctx).astype(BF)
        dqf = matmul(ds, kf_s[mine]) * (1.0 / 16.0)
        dkf = t_matmul(ds, qf_s[b])
        cosine, sine = cos_s[mine, :], sin_s[mine, :]
        for h in range(HEADS):
            dq, line = rms_back(
                qraw_s[h, mine], query_gain, turn(dqf[h * ROWS : h * ROWS + ROWS], cosine, -sine)
            )
            dq_s[h, mine] = dq.astype(BF)
            query_line = query_line + line
        dk, line = rms_back(kraw_s[mine, :], key_gain, turn(dkf, cosine, -sine))
        dkv_s[mine, 0:256] = dk.astype(BF)
        key_line = key_line + line
        tick(wide)
    h1t = h1_s[...].astype(F32).T.astype(BF)
    for h in range(HEADS):
        write_tile(grads[0], h, matmul(h1t, dq_s[h]))
    dkv_weight = matmul(h1t, dkv_s[...]).astype(BF)
    tick(wide)
    dh1 = matmul_t(dkv_s[...], kv_weight[...])
    for h in range(HEADS):
        dh1 = dh1 + matmul_t(dq_s[h], read_tile(weights[0], h))
    x = tokens[...].astype(F32)
    dx, input_line = rms_back(x, input_gain, dh1)
    grad_tokens[...] = dx1_s[...] + dx
    fill_kv_gradient(
        lambda group, part: dkv_weight[group * 80 : group * 80 + 80, part * 128 : part * 128 + 128],
        (input_line, post_attn_line, pre_ffn_line, post_ffn_line, query_line, key_line),
        grads[4],
    )
    near = [scatter(at) for at in range(3)]
    while near or wide:
        tick(near)
        tick(wide)
    exchange_out(place, sender, msgs_back, recv_back, grads)
    part_out[...] = recv_back[...]
    kv_out[...] = grads[4][place.c, place.x, place.yh, place.yl, place.z]
    sender.finish()


def run_layer(tokens, segments, cotangent, q, k, v, o_t, g, u, d_t, gains):
    vm = pl.BlockSpec(memory_space=pltpu.VMEM)
    copies = 30 + (GATHER_COPIES + SCATTER_COPIES) * len(CLASSES)
    rows = PACKS * ROWS
    scratch = [pltpu.VMEM((2, 4, 2, 2, 4, count, 128), BF) for count in BLOCK_ROWS * 2]
    scratch += [pltpu.VMEM((4, 2, 2, 4, count, 128), BF) for count in BLOCK_ROWS]
    for _, _, count, order in CLASSES:
        scratch += landing_shapes(count, order)
    scratch += [pltpu.VMEM((16, 32, 128), BF)] * 4
    scratch += [
        pltpu.VMEM((32, 128), BF),
        pltpu.VMEM((640, 512), BF),
        pltpu.VMEM((8, 640), F32),
        pltpu.VMEM((rows, 640), BF),
        pltpu.VMEM((HEADS, rows, 256), F32),
        pltpu.VMEM((rows, 256), F32),
        pltpu.VMEM((PACKS, HEADS * ROWS, 256), BF),
        pltpu.VMEM((rows, 256), BF),
        pltpu.VMEM((rows, 256), BF),
        pltpu.VMEM((PACKS, HEADS * ROWS, ROWS), F32),
        pltpu.VMEM((HEADS, rows, 256), BF),
        pltpu.VMEM((rows, 640), F32),
        pltpu.VMEM((rows, 640), F32),
        pltpu.VMEM((rows, 640), BF),
        pltpu.VMEM((8, rows, 256), F32),
        pltpu.VMEM((8, rows, 256), F32),
        pltpu.VMEM((8, rows, 256), BF),
        pltpu.VMEM((rows, 640), F32),
        pltpu.VMEM((rows, 640), BF),
        pltpu.VMEM((rows, 640), F32),
        pltpu.VMEM((rows, 640), F32),
        pltpu.VMEM((rows, 640), BF),
        pltpu.VMEM((PACKS, HEADS * ROWS, 256), BF),
        pltpu.VMEM((HEADS, rows, 256), BF),
        pltpu.VMEM((rows, 512), BF),
        pltpu.VMEM((rows, 128), F32),
        pltpu.VMEM((rows, 128), F32),
        pltpu.VMEM((640, rows), BF),
        pltpu.VMEM((640, rows), BF),
        pltpu.SemaphoreType.DMA((copies,)),
        pltpu.SemaphoreType.DMA((copies,)),
    ]
    return pl.pallas_call(
        layer_kernel,
        out_shape=(
            jax.ShapeDtypeStruct((rows, 640), BF),
            jax.ShapeDtypeStruct((rows, 640), F32),
            jax.ShapeDtypeStruct((16, 32, 128), BF),
            jax.ShapeDtypeStruct((32, 128), BF),
        ),
        in_specs=[vm] * 11,
        out_specs=(vm,) * 4,
        scratch_shapes=scratch,
        compiler_params=pltpu.CompilerParams(
            collective_id=0, has_side_effects=True, vmem_limit_bytes=60 << 20
        ),
    )(tokens, segments, cotangent, q, k, v, o_t, g, u, d_t, gains)


def finish_kernel(
    layer, grad, recv, own, layer_out, grad_out,
    q_out, k_out, v_out, o_out, g_out, u_out, d_out, *gain_outs,
):
    layer_out[...] = layer[...]
    grad_out[...] = grad[...]
    for slot in range(16):
        part = recv[slot].astype(F32)
        lanes = slice(slot * 128, slot * 128 + 128)
        narrow = slice(slot % 8 * 128, slot % 8 * 128 + 128)
        g_out[:, lanes] = part[0:5]
        u_out[:, lanes] = part[8:13]
        d_out[:, lanes] = part[16:21]
        (q_out if slot < 8 else o_out)[:, narrow] = part[24:29]
    flat = own[...].astype(F32)
    k_out[:, 0:128] = flat[0:5]
    k_out[:, 128:256] = flat[8:13]
    v_out[:, 0:128] = flat[16:21]
    v_out[:, 128:256] = flat[24:29]
    for out, row in zip(gain_outs, GAIN_ROWS):
        out[...] = flat[row : row + 1, 0 : out.shape[1]]


def finish(layer, grad, recv, own):
    vm = pl.BlockSpec(memory_space=pltpu.VMEM)
    shape = lambda *dims: jax.ShapeDtypeStruct(dims, F32)
    return pl.pallas_call(
        finish_kernel,
        out_shape=(
            jax.ShapeDtypeStruct(layer.shape, BF), shape(*grad.shape),
            shape(5, 1024), shape(5, 256), shape(5, 256), shape(5, 1024),
            shape(5, 2048), shape(5, 2048), shape(5, 2048),
            shape(1, 5), shape(1, 5), shape(1, 5), shape(1, 5), shape(1, 2), shape(1, 2),
        ),
        in_specs=[vm] * 4,
        out_specs=(vm,) * 15,
    )(layer, grad, recv, own)


def per_device(
    tokens,
    segment_ids,
    cotangent,
    query_weight,
    key_weight,
    value_weight,
    out_weight,
    gate_weight,
    up_weight,
    down_weight,
    input_gain,
    query_gain,
    key_gain,
    post_attn_gain,
    pre_ffn_gain,
    post_ffn_gain,
):
    gains = (input_gain, post_attn_gain, pre_ffn_gain, post_ffn_gain, query_gain, key_gain)
    gain_rows = jnp.stack([jnp.pad(item.astype(F32), (0, 128 - item.shape[0])) for item in gains])
    gain_rows = jnp.pad(gain_rows, ((0, 2), (0, 0)))
    layer, grad, recv, own = run_layer(
        tokens, segment_ids, cotangent, query_weight, key_weight, value_weight, out_weight.T,
        gate_weight, up_weight, down_weight.T, gain_rows,
    )
    layer, grad, qg, kg, vg, og, gg, ug, dg, ig, pa, pf, po, qn, kn = finish(layer, grad, recv, own)
    ig, pa, pf, po, qn, kn = (item.reshape(-1) for item in (ig, pa, pf, po, qn, kn))
    return (layer, grad, qg, kg, vg, og.T, gg, ug, dg.T, ig, qn, kn, pa, pf, po)


def solution(mesh):
    in_specs = (
        P("dp", None),
        P("dp", None),
        P("dp", None),
        P("dp", None),
        P("dp", None),
        P("dp", None),
        P(None, "dp"),
        P("dp", None),
        P("dp", None),
        P(None, "dp"),
        P("dp"),
        P("dp"),
        P("dp"),
        P("dp"),
        P("dp"),
        P("dp"),
    )
    out_specs = (
        P("dp", None),
        P("dp", None),
        P("dp", None),
        P("dp", None),
        P("dp", None),
        P(None, "dp"),
        P("dp", None),
        P("dp", None),
        P(None, "dp"),
        P("dp"),
        P("dp"),
        P("dp"),
        P("dp"),
        P("dp"),
        P("dp"),
    )
    return jax.shard_map(
        per_device, mesh=mesh, in_specs=in_specs, out_specs=out_specs, check_vma=False
    )
```

time: 177 us -> 124 us (0.70)
  matrix products: 34 us -> 0 us
  local copies, waits for them, and re-layouts: 26.6 us -> 2.03 us
  Pallas kernels: 101 us -> 121 us
  other arithmetic: 12.2 us -> 0.6 us
    dot_general x46 -> x0, matrix products: 34 us -> none  [the longest x14 12.4 us: product(): return jnp.dot(left, right, preferred_element_type=jnp.float32)]
    pallas_call x2, Pallas kernels: 101 us -> 121 us  [the longest x1 119 us: run_layer(): pl.pallas_call(layer_kernel, out_shape=(jax.ShapeDtypeStruct((rows, 640),...]
    unnamed x187 -> x12, local copies, waits for them, and re-layouts: 14.5 us -> 1.98 us
    concatenate x3 -> x0, other arithmetic: 3.37 us -> none  [the longest x1 1.75 us: per_device(): jnp.concatenate([outer(h_first, grad_qraw), outer(grad_attn, context)], a...]
    convert_element_type x11 -> x0, other arithmetic: 2.81 us -> none  [the longest x1 0.98 us: per_device(): upstream = cotangent.astype(F32).reshape(micro_count, row_count, feat_width)]
    squeeze x2 -> x0, local copies, waits for them, and re-layouts: 2.64 us -> none  [the longest x1 1.36 us: per_device(): gain_grads[3, :5]]
    slice x2 -> x0, local copies, waits for them, and re-layouts: 2.35 us -> none  [the longest x1 1.44 us: per_device(): lines[4, :256]]
    reduce_sum x11 -> x0, other arithmetic: 2.12 us -> none  [the longest x4 1.17 us: rms_scale(): signal * lax.rsqrt(jnp.mean(signal * signal, axis=-1, keepdims=True) + no...]
where the time goes in v2:
time: 124 us
  Pallas kernels  121 us (98%)
  local copies, waits for them, and re-layouts  2.03 us (2%)
    pallas_call x1, Pallas kernels, run_layer(): pl.pallas_call(layer_kernel, out_shape=(jax.ShapeDtypeStruct((rows, 640),...  119 us

profile of v2, /device:TPU:1, one launch (start us, length us, event | category | flops | bytes accessed | tf_op | source)
XLA Modules:
  0.0 124.2 jit_solution(7615410567811228093)
XLA Ops:
  0.6 0.0 copy-start
  0.7 0.0 copy-start.1
  0.7 0.6 copy-done
  1.3 0.0 copy-done.1
  1.3 0.0 copy-start.2
  1.3 0.0 copy-start.3
  1.3 0.6 copy-done.2
  2.0 0.0 copy-done.3
  2.0 0.0 copy-start.4
  2.0 0.0 copy-start.5
  2.0 0.6 copy-done.4
  2.7 0.0 copy-done.5
  2.7 0.6 pad_convert_fusion.gains
  3.3 118.5 %shard_map.271 = (bf16[192,640]{1,0:T(8,128)(2,1)}, f32[192,640]{1,0:T(8,128)}, bf16[16,32,128]{2,1,0:T(8,128)(2,1)}, bf16[32,128]{1,0:T(8,128)(2,1)}) custom-call(bf16[192,640]{1,0:T(8,128)(2,1)} %tokens.1, s32[2,96]{1,0:T(2,128)} %segments.1, bf16[192,640]{1,0:T(8,128)(2,1)} %cotangent.1, bf16[5,1024]{1,0:T(8,128)(2,1)} %q.1, bf16[5,256]{1,0:T(8,128)(2,1)} %k.1, ...), custom_call_target="tpu_custom_call" | custom-call | tf_op jit(solution)/shard_map/pallas_call | solution.py:775
  121.8 2.2 %shard_map.272 = (bf16[192,640]{1,0:T(8,128)(2,1)}, f32[192,640]{1,0:T(8,128)}, f32[5,1024]{1,0:T(8,128)}, f32[5,256]{1,0:T(8,128)}, f32[5,256]{1,0:T(8,128)}, /...) custom-call(bf16[192,640]{1,0:T(8,128)(2,1)} %get-tuple-element.34.l, ...), custom_call_target="tpu_custom_call" | custom-call | tf_op jit(solution)/shard_map/pallas_call | solution.py:818
  (4 shorter events, 0.0 us)
Async XLA Ops:
  0.6 0.7 copy-start
  0.7 0.7 copy-start.1
  1.3 0.7 copy-start.2
  1.3 0.7 copy-start.3
  2.0 0.7 copy-start.4
  2.0 0.7 copy-start.5

commit v3 on v2

--- a/solution.py
+++ b/solution.py
@@ -72,7 +72,10 @@
         barrier = pltpu.get_barrier_semaphore()
         for other in others:
             pl.semaphore_signal(barrier, inc=1, device_id=(other,), device_id_type=MESH)
-        pl.semaphore_wait(barrier, len(others))
+        self.greeted = len(others)
+
+    def await_greetings(self):
+        pl.semaphore_wait(pltpu.get_barrier_semaphore(), self.greeted)
 
 
 def region(select, half=None):
@@ -285,14 +288,31 @@
     ]
 
 
-def picker(part, transposed=False):
-    i = lax.broadcasted_iota(jnp.int32, (80, 512), 0)
-    j = lax.broadcasted_iota(jnp.int32, (80, 512), 1)
-    n = lax.shift_right_logical(j, 5)
-    r = lax.bitwise_and(j, 7)
-    m = lax.bitwise_and(lax.shift_right_logical(j, 3), 3)
-    hit = (m == part) & (r < 5) & (i == n * 5 + r)
-    return jnp.where(hit, 1.0, 0.0).astype(BF)
+GAIN_ROWS = (5, 13, 21, 29, 6, 14)
+PICKS = 4 * 80 + 6 * 16
+
+
+def picks(row, seat):
+    n = lax.shift_right_logical(seat, 5)
+    inner = lax.bitwise_and(seat, 31)
+    r = lax.bitwise_and(seat, 7)
+    wanted = jnp.where(r < 5, lax.shift_right_logical(inner, 3) * 80 + n * 5 + r, -1)
+    for at, target in enumerate(GAIN_ROWS):
+        wanted = jnp.where(inner == target, 320 + at * 16 + n, wanted)
+    return jnp.where(wanted == row, 1.0, 0.0).astype(BF)
+
+
+def fill_picks(pick, pick_t):
+    for first in range(0, PICKS, 32):
+        shape = (32, 512)
+        pick[first : first + 32] = picks(
+            lax.broadcasted_iota(jnp.int32, shape, 0) + first, lax.broadcasted_iota(jnp.int32, shape, 1)
+        )
+    for first in range(0, 512, 32):
+        shape = (32, PICKS)
+        pick_t[first : first + 32] = picks(
+            lax.broadcasted_iota(jnp.int32, shape, 1), lax.broadcasted_iota(jnp.int32, shape, 0) + first
+        )
 
 
 def stacked(parts):
@@ -321,43 +341,9 @@
         msgs[slot] = stacked([g[:, lanes], u[:, lanes], d[:, lanes], qo]).astype(BF)
     flat = stacked([k[:, 0:128], k[:, 128:256], v[:, 0:128], v[:, 128:256]])
     row = lax.broadcasted_iota(jnp.int32, (32, 128), 0)
-    for at, target in enumerate(GAIN_ROWS):
-        flat = jnp.where(row == target, gains[at : at + 1, :], flat)
+    for gain, target in zip(gains, GAIN_ROWS):
+        flat = jnp.where(row == target, gain, flat)
     kv_block[...] = flat.astype(BF)
-
-
-GAIN_ROWS = (5, 13, 21, 29, 6, 14)
-
-
-def spread_rows(buf, row):
-    takes = []
-    for x in range(4):
-        for yh in range(2):
-            for yl in range(2):
-                both = [
-                    jnp.concatenate(
-                        [buf[c, x, yh, yl, z, row // 8 * 8 : row // 8 * 8 + 8, :] for c in range(2)], 0
-                    )
-                    for z in range(4)
-                ]
-                takes += both
-    every = jnp.concatenate(takes, axis=0)
-    i = lax.broadcasted_iota(jnp.int32, (128, 1024), 0)
-    j = lax.broadcasted_iota(jnp.int32, (128, 1024), 1)
-    pick = jnp.where(j == i * 8 + row % 8, 1.0, 0.0).astype(BF)
-    return jnp.dot(pick, every, preferred_element_type=F32)
-
-
-def gain_line(buf, row, each, width):
-    held = spread_rows(buf, row)
-    count = lax.broadcasted_iota(jnp.int32, (128, width), 0)
-    lane = lax.broadcasted_iota(jnp.int32, (128, width), 1)
-    place_in = lane - count * each
-    r = lax.broadcasted_iota(jnp.int32, (128, width), 0)
-    rep = jnp.where(lax.rem(lane, each) == r, 1.0, 0.0).astype(BF)
-    lined = jnp.dot(held.astype(BF), rep, preferred_element_type=F32)
-    lined = jnp.where((place_in >= 0) & (place_in < each), lined, 0.0)
-    return jnp.sum(lined, axis=0, keepdims=True)
 
 
 def exchange_start(place, sender, msgs, recv):
@@ -367,60 +353,83 @@
     ]
 
 
-def exchange_take(place, copies, msgs, recv, bufs, kv_block):
+def exchange_take(place, copies, msgs, recv, bufs, kv_block, pick):
     recv[place.natural()] = msgs[place.slot()]
     spot = (place.c, place.x, place.yh, place.yl, place.z)
     bufs[4][spot] = kv_block[...]
     for copy in copies:
         copy.wait_recv()
-    flat = recv[...].reshape(512, 128)
+    flat = matmul(pick[0:320], recv[...].reshape(512, 128)).astype(BF)
     for part, buf in ((3, bufs[0]), (0, bufs[1]), (1, bufs[2]), (2, bufs[3])):
-        buf[spot] = jnp.dot(picker(part), flat, preferred_element_type=F32).astype(BF)
-
-
-def spread_gain(line, each):
-    width = line.shape[1]
-    count = lax.broadcasted_iota(jnp.int32, (128, width), 0)
-    lane = lax.broadcasted_iota(jnp.int32, (128, width), 1)
-    inside = lane - count * each
-    kept = jnp.where((inside >= 0) & (inside < each), jnp.broadcast_to(line, (128, width)), 0.0)
-    r = lax.broadcasted_iota(jnp.int32, (width, 128), 0)
-    to = lax.broadcasted_iota(jnp.int32, (width, 128), 1)
-    pick = jnp.where(lax.rem(r, each) == to, 1.0, 0.0).astype(BF)
-    return jnp.dot(kept.astype(BF), pick, preferred_element_type=F32)
-
-
-def fill_kv_gradient(kv, gain_lines, buf):
-    gains = [spread_gain(line, 5 if at < 4 else 2) for at, line in enumerate(gain_lines)]
-    row = lax.broadcasted_iota(jnp.int32, (512, 128), 0)
-    seat = lax.bitwise_and(row, 31)
-    n = lax.broadcasted_iota(jnp.int32, (512, 16), 0)
-    m = lax.broadcasted_iota(jnp.int32, (512, 16), 1)
-    repeat = jnp.where(lax.shift_right_logical(n, 5) == m, 1.0, 0.0).astype(BF)
-    for group in range(8):
-        flat = jnp.zeros((512, 128), F32)
+        buf[spot] = flat[part * 80 : part * 80 + 80]
+
+
+def read_kv(buf, pick, kv_weight, gain_parts):
+    def group(g, carry):
+        x, yh = lax.div(g, 2), lax.rem(g, 2)
+        blocks = [buf[c, x, yh, yl, z] for yl in range(2) for z in range(4) for c in range(2)]
+        parts = matmul(pick[...], jnp.concatenate(blocks, axis=0))
+        rows = pl.ds(pl.multiple_of(g * 80, 16), 80)
         for part in range(4):
-            flat = flat + lax.dot_general(
-                picker(part), kv(group, part), (((0,), (0,)), ((), ())), preferred_element_type=F32
-            )
-        for at, target in enumerate(GAIN_ROWS):
-            own = gains[at][group * 16 : group * 16 + 16].astype(BF)
-            flat = jnp.where(
-                seat == target, jnp.dot(repeat, own, preferred_element_type=F32), flat
-            )
-        flat = flat.astype(BF)
-        for n16 in range(16):
-            yl, z, c = n16 // 8, n16 // 2 % 4, n16 % 2
-            buf[c, group // 2, group % 2, yl, z] = flat[n16 * 32 : n16 * 32 + 32]
-
-
-def exchange_out(place, sender, msgs, recv, bufs):
+            kv_weight[rows, part * 128 : part * 128 + 128] = parts[
+                part * 80 : part * 80 + 80
+            ].astype(BF)
+        for at in range(6):
+            gain_parts[at, pl.ds(pl.multiple_of(g * 16, 16), 16)] = parts[
+                320 + at * 16 : 336 + at * 16
+            ]
+        return carry
+
+    lax.fori_loop(0, 8, group, 0)
+
+
+def owned(each, width):
+    n = lax.broadcasted_iota(jnp.int32, (128, width), 0)
+    inside = lax.broadcasted_iota(jnp.int32, (128, width), 1) - n * each
+    return (inside >= 0) & (inside < each)
+
+
+def seats(shape, lane_axis, each):
+    lane = lax.broadcasted_iota(jnp.int32, shape, lane_axis)
+    r = lax.broadcasted_iota(jnp.int32, shape, 1 - lane_axis)
+    return jnp.where(lax.rem(lane, each) == r, 1.0, 0.0).astype(BF)
+
+
+def read_gains(gain_parts, lines):
+    for first, count, each, width in ((0, 4, 5, 640), (4, 2, 2, 256)):
+        held = gain_parts[first : first + count].reshape(count * 128, 128).astype(BF)
+        spread = matmul(held, seats((128, width), 1, each))
+        mine = owned(each, width)
+        for at in range(count):
+            line = jnp.where(mine, spread[at * 128 : at * 128 + 128], 0.0)
+            lines[first + at : first + at + 1, 0:width] = jnp.sum(line, axis=0, keepdims=True)
+
+
+def fill_kv_gradient(kv, gain_lines, gain_parts, pick_t, buf):
+    for at, line in enumerate(gain_lines):
+        each, width = (5, 640) if at < 4 else (2, 256)
+        kept = jnp.where(owned(each, width), jnp.broadcast_to(line, (128, width)), 0.0)
+        gain_parts[at] = matmul(kept.astype(BF), seats((width, 128), 0, each))
+
+    def group(g, carry):
+        rows = pl.ds(pl.multiple_of(g * 80, 16), 80)
+        parts = [kv[rows, part * 128 : part * 128 + 128] for part in range(4)]
+        parts += [gain_parts[at, pl.ds(pl.multiple_of(g * 16, 16), 16)].astype(BF) for at in range(6)]
+        flat = matmul(pick_t[...], jnp.concatenate(parts, axis=0)).astype(BF)
+        x, yh = lax.div(g, 2), lax.rem(g, 2)
+        for n in range(16):
+            yl, z, c = n // 8, n // 2 % 4, n % 2
+            buf[c, x, yh, yl, z] = flat[n * 32 : n * 32 + 32]
+        return carry
+
+    lax.fori_loop(0, 8, group, 0)
+
+
+def exchange_out(place, sender, msgs, recv, bufs, pick_t):
     spot = (place.c, place.x, place.yh, place.yl, place.z)
-    flat = jnp.zeros((512, 128), F32)
-    for part, buf in ((3, bufs[0]), (0, bufs[1]), (1, bufs[2]), (2, bufs[3])):
-        flat = flat + lax.dot_general(
-            picker(part), buf[spot], (((0,), (0,)), ((), ())), preferred_element_type=F32
-        )
+    parts = [bufs[1][spot], bufs[2][spot], bufs[3][spot], bufs[0][spot]]
+    parts.append(jnp.zeros((PICKS - 320, 128), BF))
+    flat = matmul(pick_t[...], jnp.concatenate(parts, axis=0))
     msgs[...] = flat.astype(BF).reshape(16, 32, 128)
     copies = [
         sender.send(msgs.at[natural], recv.at[place.slot()], device)
@@ -488,19 +497,6 @@
         buf[c, :, :, yl, z + k] = value[:, k * 128 : k * 128 + 128].reshape(4, 2, 80, 128)
 
 
-def read_kv(buf, scratch):
-    def group(g, carry):
-        x, yh = lax.div(g, 2), lax.rem(g, 2)
-        blocks = [buf[c, x, yh, yl, z] for yl in range(2) for z in range(4) for c in range(2)]
-        flat = jnp.concatenate(blocks, axis=0)
-        rows = pl.ds(pl.multiple_of(g * 80, 16), 80)
-        for part in range(4):
-            scratch[rows, part * 128 : part * 128 + 128] = matmul(picker(part), flat).astype(BF)
-        return carry
-
-    lax.fori_loop(0, 8, group, 0)
-
-
 def tick(tasks):
     for task in list(tasks):
         try:
@@ -515,7 +511,8 @@
 
 
 def layer_kernel(
-    tokens, segments, cotangent, q, k, v, o, g, u, d, gains,
+    tokens, segments, cotangent, q, k, v, o, g, u, d,
+    input_gain, post_attn_gain, pre_ffn_gain, post_ffn_gain, query_gain, key_gain,
     layer_out, grad_tokens, part_out, kv_out,
     *scratch,
 ):
@@ -523,16 +520,20 @@
     scratch = scratch[15:]
     landings, scratch = scratch[: 3 * len(CLASSES)], scratch[3 * len(CLASSES) :]
     (
-        msgs, recv, msgs_back, recv_back, kv_block, kv_weight, lines,
+        msgs, recv, msgs_back, recv_back, kv_block, kv_weight, kv_weight_grad, lines,
         h1_s, qraw_s, kraw_s, qf_s, kf_s, vb_s, prob_s, ctx_s, attn_s, x1_s, h2_s,
         slope_s, gelu_s, hidden_s, mixed_s, dm_s, dh2_s, dx1_s, da_s, dctx_s, dq_s, dkv_s,
-        cos_s, sin_s, h2t_s, dmt_s,
+        cos_s, sin_s, h2t_s, dmt_s, gain_parts, pick, pick_t,
         send_sems, recv_sems,
     ) = scratch
     place = Place()
+    place.greet()
+    gains = (input_gain, post_attn_gain, pre_ffn_gain, post_ffn_gain, query_gain, key_gain)
+    gains = [jnp.pad(item[...].astype(F32)[None, :], ((0, 0), (0, 128 - item.shape[0]))) for item in gains]
     fill_messages(q, o, k, v, g, u, d, gains, msgs, kv_block)
-    place.greet()
+    fill_picks(pick, pick_t)
     sender = Sender(send_sems, recv_sems)
+    place.await_greetings()
     arrivals = exchange_start(place, sender, msgs, recv)
 
     t_of = lax.broadcasted_iota(jnp.int32, (ROWS, ROWS), 0)
@@ -549,28 +550,29 @@
         sin_s[b * ROWS : b * ROWS + ROWS] = jnp.sin(angles)
         allowed.append(same & (u_of <= t_of))
 
-    exchange_take(place, arrivals, msgs, recv, weights, kv_block)
+    exchange_take(place, arrivals, msgs, recv, weights, kv_block, pick)
 
     def gather(at):
         which, first, count, order = CLASSES[at]
         return gather_class(place, sender, weights[which], (first, count), order)
 
     near, wide = [gather(at) for at in range(3)], [gather(at) for at in range(3, 6)]
-    while near:
-        tick(near)
-        tick(wide)
-
-    read_kv(weights[4], kv_weight)
-    lines[...] = jnp.zeros((8, 640), F32)
-    for at, row in enumerate(GAIN_ROWS):
-        if at < 4:
-            lines[at : at + 1, :] = gain_line(weights[4], row, 5, 640)
-        else:
-            lines[at : at + 1, 0:256] = gain_line(weights[4], row, 2, 256)
+    tick(near)
+    tick(wide)
+    tick(near)
+    tick(wide)
+    tick(near)
+    tick(near)
+    tick(wide)
+    tick(near)
+    tick(near)
+    tick(near)
+    tick(wide)
+    read_kv(weights[4], pick, kv_weight, gain_parts)
+    read_gains(gain_parts, lines)
     input_gain, post_attn_gain = lines[0:1, :], lines[1:2, :]
     pre_ffn_gain, post_ffn_gain = lines[2:3, :], lines[3:4, :]
     query_gain, key_gain = lines[4:5, 0:256], lines[5:6, 0:256]
-    tick(wide)
 
     x = tokens[...].astype(F32)
     h1_s[...] = (x * inverse_rms(x) * input_gain).astype(BF)
@@ -676,13 +678,11 @@
     da, post_attn_line = rms_back(attn_s[...], post_attn_gain, dx1)
     da_s[...] = da.astype(BF)
     dat = da_s[...].astype(F32).T.astype(BF)
-    tick(wide)
     for h in range(HEADS):
         dctx = matmul(da_s[...], read_tile(weights[0], 4 + h)).astype(BF)
         for b in range(PACKS):
             dctx_s[b, h * ROWS : h * ROWS + ROWS] = dctx[b * ROWS : b * ROWS + ROWS]
         write_tile(grads[0], 4 + h, matmul(dat, ctx_s[h]))
-    tick(wide)
     query_line = jnp.zeros((1, 256), F32)
     key_line = jnp.zeros((1, 256), F32)
     for b in range(PACKS):
@@ -703,34 +703,39 @@
         dk, line = rms_back(kraw_s[mine, :], key_gain, turn(dkf, cosine, -sine))
         dkv_s[mine, 0:256] = dk.astype(BF)
         key_line = key_line + line
-        tick(wide)
+    tick(wide)
     h1t = h1_s[...].astype(F32).T.astype(BF)
     for h in range(HEADS):
         write_tile(grads[0], h, matmul(h1t, dq_s[h]))
-    dkv_weight = matmul(h1t, dkv_s[...]).astype(BF)
-    tick(wide)
+    near = [scatter(at) for at in range(2)]
+    tick(near)
+    kv_weight_grad[...] = matmul(h1t, dkv_s[...]).astype(BF)
     dh1 = matmul_t(dkv_s[...], kv_weight[...])
     for h in range(HEADS):
         dh1 = dh1 + matmul_t(dq_s[h], read_tile(weights[0], h))
     x = tokens[...].astype(F32)
     dx, input_line = rms_back(x, input_gain, dh1)
+    fill_kv_gradient(
+        kv_weight_grad,
+        (input_line, post_attn_line, pre_ffn_line, post_ffn_line, query_line, key_line),
+        gain_parts, pick_t, grads[4],
+    )
+    last = [scatter(2)]
+    tick(last)
+    tick(near)
+    tick(last)
+    near = near + last
     grad_tokens[...] = dx1_s[...] + dx
-    fill_kv_gradient(
-        lambda group, part: dkv_weight[group * 80 : group * 80 + 80, part * 128 : part * 128 + 128],
-        (input_line, post_attn_line, pre_ffn_line, post_ffn_line, query_line, key_line),
-        grads[4],
-    )
-    near = [scatter(at) for at in range(3)]
     while near or wide:
+        tick(wide)
         tick(near)
-        tick(wide)
-    exchange_out(place, sender, msgs_back, recv_back, grads)
+    exchange_out(place, sender, msgs_back, recv_back, grads, pick_t)
     part_out[...] = recv_back[...]
     kv_out[...] = grads[4][place.c, place.x, place.yh, place.yl, place.z]
     sender.finish()
 
 
-def run_layer(tokens, segments, cotangent, q, k, v, o_t, g, u, d_t, gains):
+def run_layer(tokens, segments, cotangent, q, k, v, o_t, g, u, d_t, *gains):
     vm = pl.BlockSpec(memory_space=pltpu.VMEM)
     copies = 30 + (GATHER_COPIES + SCATTER_COPIES) * len(CLASSES)
     rows = PACKS * ROWS
@@ -741,6 +746,7 @@
     scratch += [pltpu.VMEM((16, 32, 128), BF)] * 4
     scratch += [
         pltpu.VMEM((32, 128), BF),
+        pltpu.VMEM((640, 512), BF),
         pltpu.VMEM((640, 512), BF),
         pltpu.VMEM((8, 640), F32),
         pltpu.VMEM((rows, 640), BF),
@@ -769,6 +775,9 @@
         pltpu.VMEM((rows, 128), F32),
         pltpu.VMEM((640, rows), BF),
         pltpu.VMEM((640, rows), BF),
+        pltpu.VMEM((6, 128, 128), F32),
+        pltpu.VMEM((PICKS, 512), BF),
+        pltpu.VMEM((512, PICKS), BF),
         pltpu.SemaphoreType.DMA((copies,)),
         pltpu.SemaphoreType.DMA((copies,)),
     ]
@@ -780,13 +789,13 @@
             jax.ShapeDtypeStruct((16, 32, 128), BF),
             jax.ShapeDtypeStruct((32, 128), BF),
         ),
-        in_specs=[vm] * 11,
+        in_specs=[vm] * 16,
         out_specs=(vm,) * 4,
         scratch_shapes=scratch,
         compiler_params=pltpu.CompilerParams(
             collective_id=0, has_side_effects=True, vmem_limit_bytes=60 << 20
         ),
-    )(tokens, segments, cotangent, q, k, v, o_t, g, u, d_t, gains)
+    )(tokens, segments, cotangent, q, k, v, o_t, g, u, d_t, *gains)
 
 
 def finish_kernel(
@@ -846,12 +855,10 @@
     pre_ffn_gain,
     post_ffn_gain,
 ):
-    gains = (input_gain, post_attn_gain, pre_ffn_gain, post_ffn_gain, query_gain, key_gain)
-    gain_rows = jnp.stack([jnp.pad(item.astype(F32), (0, 128 - item.shape[0])) for item in gains])
-    gain_rows = jnp.pad(gain_rows, ((0, 2), (0, 0)))
     layer, grad, recv, own = run_layer(
         tokens, segment_ids, cotangent, query_weight, key_weight, value_weight, out_weight.T,
-        gate_weight, up_weight, down_weight.T, gain_rows,
+        gate_weight, up_weight, down_weight.T,
+        input_gain, post_attn_gain, pre_ffn_gain, post_ffn_gain, query_gain, key_gain,
     )
     layer, grad, qg, kg, vg, og, gg, ug, dg, ig, pa, pf, po, qn, kn = finish(layer, grad, recv, own)
     ig, pa, pf, po, qn, kn = (item.reshape(-1) for item in (ig, pa, pf, po, qn, kn))

time: 124 us -> 102 us (0.82)
  Pallas kernels: 121 us -> 101 us
  local copies, waits for them, and re-layouts: 2.03 us -> 0 us
    pallas_call x1, Pallas kernels: 119 us -> 99.3 us  [run_layer(): pl.pallas_call(layer_kernel, out_shape=(jax.ShapeDtypeStruct((rows, 640),...]
    unnamed x12 -> x0, local copies, waits for them, and re-layouts: 1.98 us -> none
where the time goes in v3:
time: 102 us
  Pallas kernels  101 us (99%)
    pallas_call x1, Pallas kernels, run_layer(): pl.pallas_call(layer_kernel, out_shape=(jax.ShapeDtypeStruct((rows, 640),...  99.3 us
    pallas_call x1, Pallas kernels, finish(): pl.pallas_call(finish_kernel, out_shape=(jax.ShapeDtypeStruct(layer.shape...  2.21 us

profile of v3, /device:TPU:1, one launch (start us, length us, event | category | flops | bytes accessed | tf_op | source)
XLA Modules:
  0.0 102.3 jit_solution(5459330627726679978)
XLA Ops:
  0.7 99.3 %shard_map.271 = (bf16[192,640]{1,0:T(8,128)(2,1)}, f32[192,640]{1,0:T(8,128)}, bf16[16,32,128]{2,1,0:T(8,128)(2,1)}, bf16[32,128]{1,0:T(8,128)(2,1)}) custom-call(bf16[192,640]{1,0:T(8,128)(2,1)} %tokens.1, s32[2,96]{1,0:T(2,128)} %segments.1, bf16[192,640]{1,0:T(8,128)(2,1)} %cotangent.1, bf16[5,1024]{1,0:T(8,128)(2,1)} %q.1, bf16[5,256]{1,0:T(8,128)(2,1)} %k.1, ...), custom_call_target="tpu_custom_call" | custom-call | tf_op jit(solution)/shard_map/pallas_call | solution.py:784
  100.0 2.2 %shard_map.272 = (bf16[192,640]{1,0:T(8,128)(2,1)}, f32[192,640]{1,0:T(8,128)}, f32[5,1024]{1,0:T(8,128)}, f32[5,256]{1,0:T(8,128)}, f32[5,256]{1,0:T(8,128)}, /...) custom-call(bf16[192,640]{1,0:T(8,128)(2,1)} %get-tuple-element.34.l, ...), custom_call_target="tpu_custom_call" | custom-call | tf_op jit(solution)/shard_map/pallas_call | solution.py:827

commit v4 on v3

--- a/solution.py
+++ b/solution.py
@@ -142,7 +142,7 @@
         self.open = []
 
 
-def gather_class(place, sender, ref, rows, order):
+def gather_class(place, sender, ref, rows, order, direct):
     tail = (pl.ds(rows[0], rows[1]), slice(None))
 
     def view(select, half=None):
@@ -170,6 +170,17 @@
     of_right = select_for(2, place.moved(axis, 1))
     of_left = select_for(2, place.moved(axis, 3))
     of_far = select_for(2, place.moved(axis, 2))
+    if direct:
+        sent = [push(view(mine), place.peer(axis, by)) for by in (1, 3, 2)]
+        twin = [push(view(mine), place.sibling())]
+        yield
+        for copy, part in zip(sent, (of_left, of_right, of_far)):
+            copy.wait_recv()
+            twin.append(push(view(part), place.sibling()))
+        yield
+        for copy in twin:
+            copy.wait_recv()
+        return
     r0 = push(view(mine, 0), right)
     l1 = push(view(mine, 1), left)
     r1 = push(view(mine, 1), right)
@@ -199,7 +210,7 @@
 SCATTER_COPIES = 16
 
 
-def scatter_class(place, sender, ref, twin_ref, landing, rows, order):
+def scatter_class(place, sender, ref, twin_ref, landing, rows, order, direct):
     tail = (pl.ds(rows[0], rows[1]), slice(None))
     order = order[::-1]
 
@@ -215,6 +226,9 @@
         return chosen
 
     def add(index, *others):
+        if len(others) == 1:
+            ref[index] = ref[index] + others[0]
+            return
         total = ref[index].astype(F32)
         for other in others:
             total = total + other.astype(F32)
@@ -240,28 +254,40 @@
     to_right = select_for(0, place.moved(axis, 1))
     to_left = select_for(0, place.moved(axis, 3))
     far = select_for(0, place.moved(axis, 2))
-    joined(0)
-    f0 = sender.send(ref.at[at(far, 0)], land.at[0], right)
-    f1 = sender.send(ref.at[at(far, 1)], land.at[1], left)
-    joined(1)
-    r1 = sender.send(ref.at[at(to_right, 1)], land.at[2], right)
-    joined(2)
-    l0 = sender.send(ref.at[at(to_left, 0)], land.at[3], left)
-    joined(3)
-    yield
-    f0.wait_recv()
-    add(at(to_right, 0), land[0])
-    r0 = sender.send(ref.at[at(to_right, 0)], land.at[4], right)
-    f1.wait_recv()
-    add(at(to_left, 1), land[1])
-    l1 = sender.send(ref.at[at(to_left, 1)], land.at[5], left)
-    yield
-    r1.wait_recv()
-    l0.wait_recv()
-    r0.wait_recv()
-    l1.wait_recv()
-    add(at(mine, 0), land[4], land[3])
-    add(at(mine, 1), land[2], land[5])
+    if direct:
+        sent = []
+        for which, by in enumerate((2, 1, 3)):
+            joined(which)
+            part = ref.at[at(select_for(0, place.moved(axis, by)))]
+            sent.append(sender.send(part, land.at[by - 1], place.peer(axis, by)))
+        joined(3)
+        yield
+        for copy in sent:
+            copy.wait_recv()
+        add(at(mine), land[0], land[1], land[2])
+    else:
+        joined(0)
+        f0 = sender.send(ref.at[at(far, 0)], land.at[0], right)
+        f1 = sender.send(ref.at[at(far, 1)], land.at[1], left)
+        joined(1)
+        r1 = sender.send(ref.at[at(to_right, 1)], land.at[2], right)
+        joined(2)
+        l0 = sender.send(ref.at[at(to_left, 0)], land.at[3], left)
+        joined(3)
+        yield
+        f0.wait_recv()
+        add(at(to_right, 0), land[0])
+        r0 = sender.send(ref.at[at(to_right, 0)], land.at[4], right)
+        f1.wait_recv()
+        add(at(to_left, 1), land[1])
+        l1 = sender.send(ref.at[at(to_left, 1)], land.at[5], left)
+        yield
+        r1.wait_recv()
+        l0.wait_recv()
+        r0.wait_recv()
+        l1.wait_recv()
+        add(at(mine, 0), land[4], land[3])
+        add(at(mine, 1), land[2], land[5])
     for step in (1, 2):
         axis = order[step]
         land = landing[step]
@@ -279,10 +305,12 @@
         add(at(select_for(step, place.at[axis])), land[0], land[1], land[2])
 
 
-def landing_shapes(rows, order):
+def landing_shapes(rows, order, direct):
     back = order[::-1]
     return [
-        pltpu.VMEM((6,) + half_shape(back[1:]) + (rows, 128), BF),
+        pltpu.VMEM(
+            ((3,) + whole_shape(back[1:]) if direct else (6,) + half_shape(back[1:])) + (rows, 128), BF
+        ),
         pltpu.VMEM((3,) + whole_shape(back[2:]) + (rows, 128), BF),
         pltpu.VMEM((3, rows, 128), BF),
     ]
@@ -302,12 +330,15 @@
     return jnp.where(wanted == row, 1.0, 0.0).astype(BF)
 
 
-def fill_picks(pick, pick_t):
+def fill_pick(pick):
     for first in range(0, PICKS, 32):
         shape = (32, 512)
         pick[first : first + 32] = picks(
             lax.broadcasted_iota(jnp.int32, shape, 0) + first, lax.broadcasted_iota(jnp.int32, shape, 1)
         )
+
+
+def fill_pick_t(pick_t):
     for first in range(0, 512, 32):
         shape = (32, PICKS)
         pick_t[first : first + 32] = picks(
@@ -323,12 +354,12 @@
 
 
 CLASSES = (
-    (0, 0, 32, "xyz"),
-    (0, 32, 48, "yzx"),
-    (4, 0, 32, "zxy"),
-    (1, 0, 80, "xyz"),
-    (2, 0, 80, "yzx"),
-    (3, 0, 80, "zxy"),
+    (0, 0, 32, "xyz", False, False),
+    (0, 32, 48, "yzx", False, False),
+    (4, 0, 32, "zxy", False, False),
+    (1, 0, 80, "xyz", False, False),
+    (2, 0, 80, "yzx", False, False),
+    (3, 0, 80, "zxy", False, False),
 )
 BLOCK_ROWS = (80, 80, 80, 80, 32)
 
@@ -531,7 +562,7 @@
     gains = (input_gain, post_attn_gain, pre_ffn_gain, post_ffn_gain, query_gain, key_gain)
     gains = [jnp.pad(item[...].astype(F32)[None, :], ((0, 0), (0, 128 - item.shape[0]))) for item in gains]
     fill_messages(q, o, k, v, g, u, d, gains, msgs, kv_block)
-    fill_picks(pick, pick_t)
+    fill_pick(pick)
     sender = Sender(send_sems, recv_sems)
     place.await_greetings()
     arrivals = exchange_start(place, sender, msgs, recv)
@@ -553,12 +584,13 @@
     exchange_take(place, arrivals, msgs, recv, weights, kv_block, pick)
 
     def gather(at):
-        which, first, count, order = CLASSES[at]
-        return gather_class(place, sender, weights[which], (first, count), order)
+        which, first, count, order, direct, _ = CLASSES[at]
+        return gather_class(place, sender, weights[which], (first, count), order, direct)
 
     near, wide = [gather(at) for at in range(3)], [gather(at) for at in range(3, 6)]
     tick(near)
     tick(wide)
+    fill_pick_t(pick_t)
     tick(near)
     tick(wide)
     tick(near)
@@ -630,7 +662,7 @@
         mixed_s[...] += matmul_t(hidden, read_tile(weights[3], t))
         return carry
 
-    lax.fori_loop(0, 8, feed, 0)
+    lax.fori_loop(0, 8, feed, 0, unroll=True)
 
     c = cotangent[...].astype(F32)
     mixed = mixed_s[...]
@@ -660,16 +692,16 @@
         return carry
 
     def scatter(at):
-        which, first, count, order = CLASSES[at]
+        which, first, count, order, _, direct = CLASSES[at]
         return scatter_class(
             place, sender, grads[which], twins[which], landings[3 * at : 3 * at + 3],
-            (first, count), order,
+            (first, count), order, direct,
         )
 
-    lax.fori_loop(0, 4, first_half, 0)
+    lax.fori_loop(0, 4, first_half, 0, unroll=True)
     wide = [scatter(at) for at in range(3, 6)]
     tick(wide)
-    lax.fori_loop(0, 4, second_half, 0)
+    lax.fori_loop(0, 4, second_half, 0, unroll=True)
     tick(wide)
 
     dx1_part, pre_ffn_line = rms_back(x1_s[...], pre_ffn_gain, dh2_s[...])
@@ -703,16 +735,17 @@
         dk, line = rms_back(kraw_s[mine, :], key_gain, turn(dkf, cosine, -sine))
         dkv_s[mine, 0:256] = dk.astype(BF)
         key_line = key_line + line
-    tick(wide)
     h1t = h1_s[...].astype(F32).T.astype(BF)
     for h in range(HEADS):
         write_tile(grads[0], h, matmul(h1t, dq_s[h]))
     near = [scatter(at) for at in range(2)]
     tick(near)
+    tick(wide)
     kv_weight_grad[...] = matmul(h1t, dkv_s[...]).astype(BF)
     dh1 = matmul_t(dkv_s[...], kv_weight[...])
     for h in range(HEADS):
         dh1 = dh1 + matmul_t(dq_s[h], read_tile(weights[0], h))
+    tick(near)
     x = tokens[...].astype(F32)
     dx, input_line = rms_back(x, input_gain, dh1)
     fill_kv_gradient(
@@ -722,13 +755,13 @@
     )
     last = [scatter(2)]
     tick(last)
-    tick(near)
+    tick(wide)
     tick(last)
     near = near + last
     grad_tokens[...] = dx1_s[...] + dx
     while near or wide:
+        tick(near)
         tick(wide)
-        tick(near)
     exchange_out(place, sender, msgs_back, recv_back, grads, pick_t)
     part_out[...] = recv_back[...]
     kv_out[...] = grads[4][place.c, place.x, place.yh, place.yl, place.z]
@@ -741,8 +774,8 @@
     rows = PACKS * ROWS
     scratch = [pltpu.VMEM((2, 4, 2, 2, 4, count, 128), BF) for count in BLOCK_ROWS * 2]
     scratch += [pltpu.VMEM((4, 2, 2, 4, count, 128), BF) for count in BLOCK_ROWS]
-    for _, _, count, order in CLASSES:
-        scratch += landing_shapes(count, order)
+    for _, _, count, order, _, direct in CLASSES:
+        scratch += landing_shapes(count, order, direct)
     scratch += [pltpu.VMEM((16, 32, 128), BF)] * 4
     scratch += [
         pltpu.VMEM((32, 128), BF),

time: 102 us -> 99.3 us (0.974)
  Pallas kernels: 101 us -> 98.3 us
    pallas_call x1, Pallas kernels: 99.3 us -> 96.1 us  [run_layer(): pl.pallas_call(layer_kernel, out_shape=(jax.ShapeDtypeStruct((rows, 640),...]
where the time goes in v4:
time: 99.3 us; the launch traced here: 99.1 us
  Pallas kernels  98.3 us (99%)
    pallas_call x1, Pallas kernels, run_layer(): pl.pallas_call(layer_kernel, out_shape=(jax.ShapeDtypeStruct((rows, 640),...  96.1 us
    pallas_call x1, Pallas kernels, finish(): pl.pallas_call(finish_kernel, out_shape=(jax.ShapeDtypeStruct(layer.shape...  2.21 us

profile of v4, /device:TPU:1, one launch (start us, length us, event | category | flops | bytes accessed | tf_op | source)
XLA Modules:
  0.0 99.1 jit_solution(12791561185769224377)
XLA Ops:
  0.7 96.1 %shard_map.271 = (bf16[192,640]{1,0:T(8,128)(2,1)}, f32[192,640]{1,0:T(8,128)}, bf16[16,32,128]{2,1,0:T(8,128)(2,1)}, bf16[32,128]{1,0:T(8,128)(2,1)}) custom-call(bf16[192,640]{1,0:T(8,128)(2,1)} %tokens.1, s32[2,96]{1,0:T(2,128)} %segments.1, bf16[192,640]{1,0:T(8,128)(2,1)} %cotangent.1, bf16[5,1024]{1,0:T(8,128)(2,1)} %q.1, bf16[5,256]{1,0:T(8,128)(2,1)} %k.1, ...), custom_call_target="tpu_custom_call" | custom-call | tf_op jit(solution)/shard_map/pallas_call | solution.py:817
  96.7 2.2 %shard_map.272 = (bf16[192,640]{1,0:T(8,128)(2,1)}, f32[192,640]{1,0:T(8,128)}, f32[5,1024]{1,0:T(8,128)}, f32[5,256]{1,0:T(8,128)}, f32[5,256]{1,0:T(8,128)}, /...) custom-call(bf16[192,640]{1,0:T(8,128)(2,1)} %get-tuple-element.34.l, ...), custom_call_target="tpu_custom_call" | custom-call | tf_op jit(solution)/shard_map/pallas_call | solution.py:860

commit v5 on v4

--- a/solution.py
+++ b/solution.py
@@ -659,13 +659,14 @@
         slope_s[t] = up * slope
         hidden = (gelu * up).astype(BF)
         hidden_s[t] = hidden
-        mixed_s[...] += matmul_t(hidden, read_tile(weights[3], t))
         return carry
 
     lax.fori_loop(0, 8, feed, 0, unroll=True)
 
     c = cotangent[...].astype(F32)
-    mixed = mixed_s[...]
+    mixed = matmul_t(hidden_s[0], read_tile(weights[3], 0))
+    for t in range(1, 8):
+        mixed = mixed + matmul_t(hidden_s[t], read_tile(weights[3], t))
     layer_out[...] = (x1_s[...] + mixed * inverse_rms(mixed) * post_ffn_gain).astype(BF)
     dm, post_ffn_line = rms_back(mixed, post_ffn_gain, c)
     dm_s[...] = dm.astype(BF)

time: 99.3 us -> 97.8 us (0.985)
  Pallas kernels: 98.3 us -> 96.8 us
    pallas_call x1, Pallas kernels: 96.1 us -> 94.6 us  [run_layer(): pl.pallas_call(layer_kernel, out_shape=(jax.ShapeDtypeStruct((rows, 640),...]
where the time goes in v5:
time: 97.8 us; the launch traced here: 97.6 us
  Pallas kernels  96.8 us (99%)
    pallas_call x1, Pallas kernels, run_layer(): pl.pallas_call(layer_kernel, out_shape=(jax.ShapeDtypeStruct((rows, 640),...  94.6 us
    pallas_call x1, Pallas kernels, finish(): pl.pallas_call(finish_kernel, out_shape=(jax.ShapeDtypeStruct(layer.shape...  2.21 us

profile of v5, /device:TPU:1, one launch (start us, length us, event | category | flops | bytes accessed | tf_op | source)
XLA Modules:
  0.0 97.6 jit_solution(3657502418464199214)
XLA Ops:
  0.7 94.6 %shard_map.271 = (bf16[192,640]{1,0:T(8,128)(2,1)}, f32[192,640]{1,0:T(8,128)}, bf16[16,32,128]{2,1,0:T(8,128)(2,1)}, bf16[32,128]{1,0:T(8,128)(2,1)}) custom-call(bf16[192,640]{1,0:T(8,128)(2,1)} %tokens.1, s32[2,96]{1,0:T(2,128)} %segments.1, bf16[192,640]{1,0:T(8,128)(2,1)} %cotangent.1, bf16[5,1024]{1,0:T(8,128)(2,1)} %q.1, bf16[5,256]{1,0:T(8,128)(2,1)} %k.1, ...), custom_call_target="tpu_custom_call" | custom-call | tf_op jit(solution)/shard_map/pallas_call | solution.py:818
  95.3 2.2 %shard_map.272 = (bf16[192,640]{1,0:T(8,128)(2,1)}, f32[192,640]{1,0:T(8,128)}, f32[5,1024]{1,0:T(8,128)}, f32[5,256]{1,0:T(8,128)}, f32[5,256]{1,0:T(8,128)}, /...) custom-call(bf16[192,640]{1,0:T(8,128)(2,1)} %get-tuple-element.34.l, ...), custom_call_target="tpu_custom_call" | custom-call | tf_op jit(solution)/shard_map/pallas_call | solution.py:861
